TPU v7x, 256 devices: a whole 4x4x8 slice. The times are simulated.
256 devices in a mesh: table: 32 (over y, z), tensor: 8 (over x, core).
Axes of the slice: x: 4, y: 4, z: 8, core: 2. Of those that a mesh axis runs over, the one named last changes fastest.
Arguments:
- table_rows: bfloat16 [131072, 256], P('table'), may hold values from -60 to 60
- hist_owner: int32 [64, 512], P('table', 'tensor'), may hold values from 0 to 31, as said below
- hist_row: int32 [64, 512], P('table', 'tensor'), may hold values from 0 to 4095
- ln_gain: float32 [256], replicated, may hold values from 0.1 to 1.9
- w_proj: bfloat16 [256, 16, 256], P(None, 'tensor'), may hold values from -0.375 to 0.375
- norm_gain: float32 [16, 64], P('tensor'), may hold values from 0.1 to 1.9
- w_out: bfloat16 [16, 64, 256], P('tensor'), may hold values from -0.1875 to 0.1875
- w_ckv: bfloat16 [256, 16, 128], P(None, 'tensor'), may hold values from -0.375 to 0.375
- candidates: bfloat16 [16384, 256], P('table'), may hold values from -6 to 6
- cand_group: int32 [128], P('table'), may hold values from 0 to 31, as said below
- cand_member: int32 [128], P('table'), may hold values from 0 to 1
- block_mask: int32 [128, 4], P('table'), may hold values 0 or 1
- w_cq: bfloat16 [256, 16, 64], P(None, 'tensor'), may hold values from -0.375 to 0.375
- w_co: bfloat16 [16, 64, 256], P('tensor'), may hold values from -0.1875 to 0.1875
- w_mlp: bfloat16 [256, 1024], P(None, 'tensor'), may hold values from -0.375 to 0.375
- w_score: bfloat16 [1024], P('tensor'), may hold values from -0.1875 to 0.1875
Outputs:
- states: bfloat16 [64, 512, 256], P('table', 'tensor')
- scores: float32 [16384], P('table')
Inputs may be any that keep to these rules, and one draw needn't show every extreme that they name: `hist_owner`: in each device's block of 2 users by 64 positions, at most 8 entries name one slab. `cand_group`: among the 4 candidate blocks of one index of table, at most 1 name one group.
All inputs are finite; a program needn't handle non-finite values. No bound on the sum of `block_mask` on one device may be relied on, other than what follows from the above.
Results may differ from a plain program's by a relative error of at most 0.017.
Values may be sent and summed in bfloat16 or wider, within the bound.
A program may use at most 64 MiB of HBM per device.

v0:
```python
import math

import jax
import jax.numpy as jnp
from jax import lax
from jax.sharding import PartitionSpec as P


def normalize(values_f32, gain_vec):
    mean_val = jnp.mean(values_f32, axis=-1, keepdims=True)
    centred = values_f32 - mean_val
    var_val = jnp.mean(centred * centred, axis=-1, keepdims=True)
    return centred * lax.rsqrt(var_val + 1e-05) * gain_vec


def fetch_rows(table_rows, owner_ids, row_ids):
    slab_count = lax.axis_size("table")
    user_count, position_count = owner_ids.shape
    request_count = user_count * position_count
    flat_owner = owner_ids.reshape(request_count)
    flat_row = row_ids.reshape(request_count)
    capacity = 2 * request_count // slab_count
    one_hot = (flat_owner[:, None] == jnp.arange(slab_count, dtype=jnp.int32)[None, :]).astype(
        jnp.int32
    )
    earlier = jnp.sum((jnp.cumsum(one_hot, axis=0) - one_hot) * one_hot, axis=1)
    slot_index = flat_owner * capacity + earlier
    wanted = (
        jnp.zeros((slab_count * capacity,), jnp.int32)
        .at[slot_index]
        .set(flat_row)
        .reshape(slab_count, capacity)
    )
    looked_up = jnp.take(
        table_rows, lax.all_to_all(wanted, "table", split_axis=0, concat_axis=0, tiled=True), axis=0
    )
    replies = lax.all_to_all(looked_up, "table", split_axis=0, concat_axis=0, tiled=True)
    fetched = jnp.take(replies.reshape(slab_count * capacity, -1), slot_index, axis=0)
    return fetched.reshape(user_count, position_count, -1)


def causal_attention(queries, keys, values):
    user_count, hist_len, head_local, head_size = queries.shape
    block_len = min(512, hist_len)
    scale_head = 1.0 / math.sqrt(head_size)
    positions = jnp.arange(hist_len)

    def one_block(block_start):
        scores = (
            jnp.einsum("uqhd,ukhd->uhqk", queries, keys, preferred_element_type=jnp.float32)
            * scale_head
        )
        allowed = positions[None, :] <= (block_start + jnp.arange(block_len))[:, None]
        weights = jnp.where(allowed[None, None], jax.nn.silu(scores), 0.0).astype(jnp.bfloat16)
        return jnp.einsum("uhqk,ukhd->uqhd", weights, values, preferred_element_type=jnp.float32)

    starts = jnp.arange(hist_len // block_len) * block_len
    pieces = lax.map(one_block, starts)
    return jnp.moveaxis(pieces, 0, 1).reshape(user_count, hist_len, head_local, head_size)


def body(
    table_rows,
    hist_owner,
    hist_row,
    ln_gain,
    w_proj,
    norm_gain,
    w_out,
    w_ckv,
    candidates,
    cand_group,
    cand_member,
    block_mask,
    w_cq,
    w_co,
    w_mlp,
    w_score,
):
    slab_count = lax.axis_size("table")
    piece_len = hist_owner.shape[1]
    owner_all, row_all = (
        lax.all_gather(hist_owner, "tensor", axis=1, tiled=True),
        lax.all_gather(hist_row, "tensor", axis=1, tiled=True),
    )
    history = fetch_rows(table_rows, owner_all, row_all)
    hist_len = history.shape[1]
    head_size = w_proj.shape[2] // 4
    head_local = w_proj.shape[1]
    scale_head = 1.0 / math.sqrt(head_size)
    scale_hist = 1.0 / math.sqrt(hist_len)
    rows_f32 = history.astype(jnp.float32)
    normed = normalize(rows_f32, ln_gain).astype(jnp.bfloat16)
    projected = jax.nn.silu(
        jnp.einsum("utd,dhe->uthe", normed, w_proj, preferred_element_type=jnp.float32)
    ).astype(jnp.bfloat16)
    gate_u = projected[..., :head_size]
    values = projected[..., head_size : 2 * head_size]
    queries = projected[..., 2 * head_size : 3 * head_size]
    keys = projected[..., 3 * head_size :]
    attended = causal_attention(queries, keys, values)
    gated = (normalize(attended, norm_gain) * gate_u.astype(jnp.float32)).astype(jnp.bfloat16)
    partial_out = jnp.einsum("uthe,hed->utd", gated, w_out, preferred_element_type=jnp.float32)
    piece_start = lax.axis_index("tensor") * piece_len
    head_total = lax.psum(partial_out, "tensor")
    states = (rows_f32 + head_total).astype(jnp.bfloat16)
    states_out = lax.dynamic_slice_in_dim(states, piece_start, piece_len, 1)
    cross_kv = jnp.einsum(
        "usd,dhe->ushe", states, w_ckv, preferred_element_type=jnp.float32
    ).astype(jnp.bfloat16)
    block_count = cand_group.shape[0]
    block_cap = max(1, 2 * block_count // slab_count)
    cand_rows = candidates.shape[0] // block_count
    mask_blocks = block_mask.shape[1]
    cand_queries = jnp.einsum(
        "cd,dhe->che", candidates, w_cq, preferred_element_type=jnp.float32
    ).astype(jnp.bfloat16)
    query_blocks = cand_queries.reshape(block_count, cand_rows, head_local * head_size)
    group_hot = (cand_group[:, None] == jnp.arange(slab_count, dtype=jnp.int32)[None, :]).astype(
        jnp.int32
    )
    before = jnp.sum((jnp.cumsum(group_hot, axis=0) - group_hot) * group_hot, axis=1)
    block_slot = cand_group * block_cap + before
    slot_total = slab_count * block_cap
    send_queries = (
        jnp.zeros((slot_total, cand_rows, head_local * head_size), jnp.bfloat16)
        .at[block_slot]
        .set(query_blocks)
        .reshape(slab_count, block_cap, cand_rows, head_local * head_size)
    )
    send_member = (
        jnp.zeros((slot_total,), jnp.int32)
        .at[block_slot]
        .set(cand_member)
        .reshape(slab_count, block_cap)
    )
    send_mask = (
        jnp.zeros((slot_total, mask_blocks), jnp.int32)
        .at[block_slot]
        .set(block_mask)
        .reshape(slab_count, block_cap, mask_blocks)
    )
    query_in = lax.all_to_all(send_queries, "table", split_axis=0, concat_axis=0, tiled=True)
    member_in = lax.all_to_all(send_member, "table", split_axis=0, concat_axis=0, tiled=True)
    mask_in = lax.all_to_all(send_mask, "table", split_axis=0, concat_axis=0, tiled=True)
    sources, taken = member_in.shape
    total_slots = sources * taken
    group_len = math.gcd(total_slots, 8)
    group_count = total_slots // group_len
    grouped = (
        query_in.reshape(group_count, group_len, cand_rows, head_local, head_size),
        member_in.reshape(group_count, group_len),
        mask_in.reshape(group_count, group_len, mask_blocks),
    )

    def one_group(items):
        query_group, member_group, mask_group = items
        selected = jnp.take(cross_kv, member_group, axis=0)
        keys_sel = selected[..., :head_size]
        values_sel = selected[..., head_size:]
        scores = (
            jnp.einsum("gchd,gkhd->ghck", query_group, keys_sel, preferred_element_type=jnp.float32)
            * scale_head
        )
        position_mask = jnp.repeat(mask_group, hist_len // mask_blocks, axis=1).astype(jnp.float32)
        weights = (jax.nn.silu(scores) * position_mask[:, None, None, :] * scale_hist).astype(
            jnp.bfloat16
        )
        return jnp.einsum(
            "ghck,gkhd->gchd", weights, values_sel, preferred_element_type=jnp.float32
        ).astype(jnp.bfloat16)

    answered = lax.map(one_group, grouped).reshape(
        sources, taken, cand_rows, head_local * head_size
    )
    returned = lax.all_to_all(answered, "table", split_axis=0, concat_axis=0, tiled=True)
    cross = jnp.take(
        returned.reshape(slot_total, cand_rows, head_local * head_size), block_slot, axis=0
    )
    cross = cross.reshape(block_count * cand_rows, head_local, head_size)
    partial_cross = jnp.einsum("che,hed->cd", cross, w_co, preferred_element_type=jnp.float32)
    cross_total = lax.psum(partial_cross, "tensor")
    mixed = (candidates.astype(jnp.float32) + cross_total).astype(jnp.bfloat16)
    hidden = jax.nn.silu(jnp.dot(mixed, w_mlp, preferred_element_type=jnp.float32)).astype(
        jnp.bfloat16
    )
    partial_score = jnp.dot(hidden, w_score, preferred_element_type=jnp.float32)
    scores_out = lax.psum(partial_score, "tensor")
    return (states_out, scores_out)


def solution(mesh):
    return jax.shard_map(
        body,
        mesh=mesh,
        in_specs=(
            P("table", None),
            P("table", "tensor"),
            P("table", "tensor"),
            P(),
            P(None, "tensor", None),
            P("tensor", None),
            P("tensor", None, None),
            P(None, "tensor", None),
            P("table", None),
            P("table"),
            P("table"),
            P("table", None),
            P(None, "tensor", None),
            P("tensor", None, None),
            P(None, "tensor"),
            P("tensor"),
        ),
        out_specs=(P("table", "tensor", None), P("table")),
        check_vma=False,
    )
```

profile of v0, /device:TPU:1, one launch (start us, length us, event | category | flops | bytes accessed | tf_op | source)
XLA Modules:
  0.0 399.7 jit_solution(2262217798121501004)
XLA Ops:
  7.2 12.2 %all-gather = s32[8,64,2]{1,2,0:T(2,128)S(1)} all-gather(s32[1,64,2]{1,2,0:T(2,128)} %bitcast.161), channel_id=1, replica_groups=mesh['table'=32,'tensor'=8] {'tensor'}, dimensions={0}, use_global_device_ids=true | all-gather | bytes 4608 | tf_op jit(solution)/shard_map/all_gather | solution.py:83
  19.6 9.0 %reduce-window.6 = s32[32,8,128]{2,1,0:T(8,128)S(1)} reduce-window(s32[32,8,128]{2,1,0:T(8,128)S(1)} %fusion.51, s32[]{:T(128)} %constant.97.clone.1), window={size=1x1x128 pad=0_0x0_0x127_0}, to_apply=%region_0.0 | reduce-window | flops 4161536 | bytes 262148 | tf_op jit(solution)/shard_map/reduce-window
  28.7 0.1 copy.95
  29.0 9.0 %all-gather.1 = s32[8,64,2]{1,2,0:T(2,128)S(1)} all-gather(s32[1,64,2]{1,2,0:T(2,128)} %bitcast.162), channel_id=1, replica_groups=mesh['table'=32,'tensor'=8] {'tensor'}, dimensions={0}, use_global_device_ids=true | all-gather | bytes 4608 | tf_op jit(solution)/shard_map/all_gather | solution.py:84
  38.2 4.3 %scatter_custom_fusion = s32[2048]{0:T(1024)S(1)} fusion(s32[1024]{0:T(1024)S(1)} %bitcast.154, s32[1024]{0:T(1024)S(1)} %bitcast.159, s32[]{:T(128)} %constant.97.clone.1), kind=kCustom, calls=%fused_computation.99 | custom fusion | bytes 8196 | tf_op jit(solution)/shard_map/scatter | solution.py:31
  42.6 19.0 %all_to_all.44 = s32[32,1,64]{2,1,0:T(1,128)S(1)} all-to-all(s32[32,1,64]{2,1,0:T(1,128)S(1)} %all_to_all.28), channel_id=1, replica_groups=mesh['table'=32,'tensor'=8] {'table'}, dimensions={0} | all-to-all | bytes 16384 | tf_op jit(solution)/shard_map/all_to_all | solution.py:35
  61.7 7.5 %gather_fusion.1 = bf16[2048,256]{1,0:T(8,128)(2,1)S(1)} fusion(bf16[4096,256]{1,0:T(8,128)(2,1)S(1)} %copy-done, s32[2048]{0:T(1024)S(1)} %broadcast_clamp_fusion), kind=kCustom, calls=%fused_computation.1 | custom fusion | bytes 2105344 | tf_op jit(solution)/shard_map/jit(_take)/gather | solution.py:34
  69.2 1.3 broadcast_select_fusion.1
  70.5 3.9 all-to-all-start.1
  74.5 0.9 copy.98
  75.5 0.2 select_reduce_fusion
  75.7 0.7 scatter_custom_fusion.1
  76.4 0.7 copy.99
  77.1 1.2 fusion.74
  78.3 0.1 copy.101
  78.5 1.3 scatter_custom_fusion.3
  79.8 1.2 broadcast_in_dim.130
  81.0 2.0 scatter_fusion
  83.1 16.0 %all-to-all-done.1 = bf16[32,64,256]{2,1,0:T(8,128)(2,1)S(1)} async-done(((bf16[32,64,256]{2,1,0:T(8,128)(2,1)}), bf16[32,64,256]{2,1,0:T(8,128)(2,1)S(1)}, u32[]{:S(2)}, u32[]{:S(2)}) %all-to-all-start.1) | async-done | bytes 1048608 | tf_op jit(solution)/shard_map/all_to_all | solution.py:37
  99.1 8.5 %all-to-all-start.2 = ((s32[32,1,1]{2,1,0:T(1,128)}), s32[32,1,1]{2,1,0:T(1,128)S(1)}, u32[]{:S(2)}, u32[]{:S(2)}) async-start(s32[32,1,1]{2,1,0:T(1,128)} %copy.99), calls=%async_computation.2 | async-start | bytes 32768 | tf_op jit(solution)/shard_map/all_to_all | solution.py:144
  107.6 4.9 %gather_fusion.2 = bf16[1024,256]{1,0:T(8,128)(2,1)} fusion(bf16[2048,256]{1,0:T(8,128)(2,1)S(1)} %bitcast.137, s32[1024]{0:T(1024)S(1)} %broadcast_clamp_fusion.1), kind=kCustom, calls=%fused_computation.2 | custom fusion | bytes 1052672 | tf_op jit(solution)/shard_map/jit(_take)/gather | solution.py:38
  112.6 1.5 convert_reduce_fusion
  114.1 1.5 fusion.24
  115.6 0.6 all-to-all-done.2
  116.2 8.7 %all-to-all-start.4 = ((s32[32,1,4]{2,1,0:T(1,128)}), s32[32,1,4]{2,1,0:T(1,128)S(1)}, u32[]{:S(2)}, u32[]{:S(2)}) async-start(s32[32,1,4]{2,1,0:T(1,128)} %bitcast.53), calls=%async_computation.4 | async-start | bytes 32768 | tf_op jit(solution)/shard_map/all_to_all | solution.py:145
  124.9 8.6 %all-to-all-done.4 = s32[32,1,4]{2,1,0:T(1,128)S(1)} async-done(((s32[32,1,4]{2,1,0:T(1,128)}), s32[32,1,4]{2,1,0:T(1,128)S(1)}, u32[]{:S(2)}, u32[]{:S(2)}) %all-to-all-start.4) | async-done | bytes 544 | tf_op jit(solution)/shard_map/all_to_all | solution.py:145
  133.5 4.7 %all-to-all-start.3 = ((bf16[32,1,128,128]{3,2,1,0:T(8,128)(2,1)}), bf16[32,1,128,128]{3,2,1,0:T(8,128)(2,1)}, u32[]{:S(2)}, u32[]{:S(2)}) async-start(bf16[32,1,128,128]{3,2,1,0:T(8,128)(2,1)} %bitcast.140), calls=%async_computation.3 | async-start | bytes 2097152 | tf_op jit(solution)/shard_map/all_to_all | solution.py:143
  138.2 0.2 all-reduce.3.cloned.1.call-start
  138.4 2.2 multiply_convert_fusion.1
  140.7 3.1 fusion.69
  143.9 2.4 convolution_bitcast_fusion
  146.3 0.7 reduce.2
  147.2 12.7 %all-to-all-done.3 = bf16[32,1,128,128]{3,2,1,0:T(8,128)(2,1)} async-done(((bf16[32,1,128,128]{3,2,1,0:T(8,128)(2,1)}), bf16[32,1,128,128]{3,2,1,0:T(8,128)(2,1)}, u32[]{:S(2)}, u32[]{:S(2)}) %all-to-all-start.3) | async-done | bytes 1048608 | tf_op jit(solution)/shard_map/all_to_all | solution.py:143
  159.8 2.3 copy.103
  162.1 52.2 %all-reduce.3.cloned.1.call-done = f32[2,512,256]{2,1,0:T(8,128)} async-done(((f32[2,512,256]{2,1,0:T(8,128)}), f32[2,512,256]{2,1,0:T(8,128)}) %all-reduce.3.cloned.1.call-update) | async-done | bytes 1048592 | tf_op jit(solution)/shard_map/psum | solution.py:105
  214.3 1.4 fusion.22
  215.8 0.3 convolution_convert_fusion
  216.1 55.2 %while.2 = (s32[]{:T(128)}, bf16[4,8,128,2,64]{2,4,3,1,0:T(8,128)(2,1)}, s32[4,8]{1,0:T(4,128)S(1)}, bf16[2,512,2,128]{3,1,2,0:T(8,128)(2,1)S(1)}, bf16[4,8,128,...) while((s32[]{:T(128)}, bf16[4,8,128,2,64]{2,4,3,1,0:T(8,128)(2,1)}, ...), condition=%wide.region_15.16_spmd, body=%wide.region_14.15_spmd.sunk | while | flops 278004832 | bytes 15242897 | solution.py:173
  216.2 2.2 gather_fusion
  218.4 3.9 copy.127
  222.3 3.1 broadcast_select_fusion.6
  225.5 4.4 %fusion.88 = bf16[4,8,128,2,64]{2,4,3,1,0:T(8,128)(2,1)} fusion(bf16[4,8,128,2,64]{2,4,3,1,0:T(8,128)(2,1)} %get-tuple-element.156, s32[]{:T(128)S(6)} %copy.133, f32[8,512]{1,0:T(8,128)S(1)} %broadcast_bitcast_fusion.3, bf16[8,512,2,128]{1,3,2,0:T(8,128)(2,1)} %broadcast_select_fusion.6, bf16[4,8,128,2,64]{2,4,3,1,0:T(8,128)(2,1)} %get-tuple-element.166), kind=kOutput, calls=%fused_computation.13.clone.1 | convolution fusion | flops 276955136 | bytes 2638848 | tf_op jit(solution)/shard_map/while/body/eval_jaxpr/ghck,gkhd->gchd/dot_general | solution.py:169
  230.0 2.2 gather_fusion
  232.2 3.9 copy.127
  236.1 3.1 broadcast_select_fusion.6
  239.2 4.5 %fusion.88 = bf16[4,8,128,2,64]{2,4,3,1,0:T(8,128)(2,1)} fusion(bf16[4,8,128,2,64]{2,4,3,1,0:T(8,128)(2,1)} %get-tuple-element.156, s32[]{:T(128)S(6)} %copy.133, f32[8,512]{1,0:T(8,128)S(1)} %broadcast_bitcast_fusion.3, bf16[8,512,2,128]{1,3,2,0:T(8,128)(2,1)} %broadcast_select_fusion.6, bf16[4,8,128,2,64]{2,4,3,1,0:T(8,128)(2,1)} %get-tuple-element.166), kind=kOutput, calls=%fused_computation.13.clone.1 | convolution fusion | flops 276955136 | bytes 2638848 | tf_op jit(solution)/shard_map/while/body/eval_jaxpr/ghck,gkhd->gchd/dot_general | solution.py:169
  243.8 2.2 gather_fusion
  246.0 3.9 copy.127
  249.9 3.1 broadcast_select_fusion.6
  253.0 4.4 %fusion.88 = bf16[4,8,128,2,64]{2,4,3,1,0:T(8,128)(2,1)} fusion(bf16[4,8,128,2,64]{2,4,3,1,0:T(8,128)(2,1)} %get-tuple-element.156, s32[]{:T(128)S(6)} %copy.133, f32[8,512]{1,0:T(8,128)S(1)} %broadcast_bitcast_fusion.3, bf16[8,512,2,128]{1,3,2,0:T(8,128)(2,1)} %broadcast_select_fusion.6, bf16[4,8,128,2,64]{2,4,3,1,0:T(8,128)(2,1)} %get-tuple-element.166), kind=kOutput, calls=%fused_computation.13.clone.1 | convolution fusion | flops 276955136 | bytes 2638848 | tf_op jit(solution)/shard_map/while/body/eval_jaxpr/ghck,gkhd->gchd/dot_general | solution.py:169
  257.6 2.2 gather_fusion
  259.8 3.9 copy.127
  263.7 3.1 broadcast_select_fusion.6
  266.8 4.4 %fusion.88 = bf16[4,8,128,2,64]{2,4,3,1,0:T(8,128)(2,1)} fusion(bf16[4,8,128,2,64]{2,4,3,1,0:T(8,128)(2,1)} %get-tuple-element.156, s32[]{:T(128)S(6)} %copy.133, f32[8,512]{1,0:T(8,128)S(1)} %broadcast_bitcast_fusion.3, bf16[8,512,2,128]{1,3,2,0:T(8,128)(2,1)} %broadcast_select_fusion.6, bf16[4,8,128,2,64]{2,4,3,1,0:T(8,128)(2,1)} %get-tuple-element.166), kind=kOutput, calls=%fused_computation.13.clone.1 | convolution fusion | flops 276955136 | bytes 2638848 | tf_op jit(solution)/shard_map/while/body/eval_jaxpr/ghck,gkhd->gchd/dot_general | solution.py:169
  271.3 2.3 copy.108
  273.6 9.8 %all-to-all-start.5 = ((bf16[32,1,128,128]{3,2,1,0:T(8,128)(2,1)}), bf16[32,1,128,128]{3,2,1,0:T(8,128)(2,1)}, u32[]{:S(2)}, u32[]{:S(2)}) async-start(bf16[32,1,128,128]{3,2,1,0:T(8,128)(2,1)} %copy.108), calls=%async_computation.5 | async-start | bytes 2097152 | tf_op jit(solution)/shard_map/all_to_all | solution.py:176
  283.6 23.2 %all-to-all-done.5 = bf16[32,1,128,128]{3,2,1,0:T(8,128)(2,1)} async-done(((bf16[32,1,128,128]{3,2,1,0:T(8,128)(2,1)}), bf16[32,1,128,128]{3,2,1,0:T(8,128)(2,1)}, u32[]{:S(2)}, u32[]{:S(2)}) %all-to-all-start.5) | async-done | bytes 1048608 | tf_op jit(solution)/shard_map/all_to_all | solution.py:176
  306.8 1.8 gather_fusion.3
  308.6 0.1 copy.109
  308.8 1.1 convolution_bitcast_fusion.1
  309.9 0.6 constant_dynamic-slice_fusion.1
  310.5 65.9 %all-reduce.5.cloned.1.call-done = f32[512,256]{1,0:T(8,128)} async-done(((f32[512,256]{1,0:T(8,128)}), f32[512,256]{1,0:T(8,128)}) %all-reduce.5.cloned.1.call-update) | async-done | bytes 524304 | tf_op jit(solution)/shard_map/psum | solution.py:182
  376.4 1.4 fusion.39
  377.8 15.0 %psum.23 = f32[512]{0:T(512)} all-reduce(f32[512]{0:T(512)S(1)} %bitcast.160), channel_id=1, replica_groups=mesh['table'=32,'tensor'=8] {'tensor'}, use_global_device_ids=true, to_apply=%region_17.18 | all-reduce | flops 512 | bytes 4096 | tf_op jit(solution)/shard_map/psum | solution.py:188
  (96 shorter events, 2.0 us)
Async XLA Ops:
  7.2 54.5 %copy-start = (bf16[4096,256]{1,0:T(8,128)(2,1)S(1)}, bf16[4096,256]{1,0:T(8,128)(2,1)}, u32[]{:S(2)}) copy-start(bf16[4096,256]{1,0:T(8,128)(2,1)} %param.18) | copy-start | bytes 6291460
  69.2 5.3 %copy-start.2 = (bf16[256,2,256]{2,1,0:T(2,128)(2,1)S(1)}, bf16[256,2,256]{2,1,0:T(2,128)(2,1)}, u32[]{:S(2)}) copy-start(bf16[256,2,256]{2,1,0:T(2,128)(2,1)} %param.22) | copy-start | bytes 786436
  69.2 6.2 %copy-start.9 = (s32[4]{0:T(128)S(1)}, s32[4]{0:T(128)}, u32[]{:S(2)}) copy-start(s32[4]{0:T(128)} %param.27) | copy-start | bytes 52
  69.2 7.9 %copy-start.6 = (bf16[256,2,64]{0,2,1:T(8,128)(2,1)S(1)}, bf16[256,2,64]{0,2,1:T(8,128)(2,1)}, u32[]{:S(2)}) copy-start(bf16[256,2,64]{0,2,1:T(8,128)(2,1)} %param.30) | copy-start | bytes 196612
  70.5 28.6 %all-to-all-start.1 = ((bf16[32,64,256]{2,1,0:T(8,128)(2,1)}), bf16[32,64,256]{2,1,0:T(8,128)(2,1)S(1)}, u32[]{:S(2)}, u32[]{:S(2)}) async-start(bf16[32,64,256]{2,1,0:T(8,128)(2,1)} %broadcast_select_fusion.1), calls=%async_computation.1 | async-start | bytes 2097152 | tf_op jit(solution)/shard_map/all_to_all | solution.py:37
  99.1 17.1 %all-to-all-start.2 = ((s32[32,1,1]{2,1,0:T(1,128)}), s32[32,1,1]{2,1,0:T(1,128)S(1)}, u32[]{:S(2)}, u32[]{:S(2)}) async-start(s32[32,1,1]{2,1,0:T(1,128)} %copy.99), calls=%async_computation.2 | async-start | bytes 32768 | tf_op jit(solution)/shard_map/all_to_all | solution.py:144
  112.6 25.8 %copy-start.1 = (bf16[1024,256]{1,0:T(8,128)(2,1)S(1)}, bf16[1024,256]{1,0:T(8,128)(2,1)}, u32[]{:S(2)}) copy-start(bf16[1024,256]{1,0:T(8,128)(2,1)} %gather_fusion.2) | copy-start | bytes 1572868
  112.6 25.8 %copy-start.4 = (bf16[256,2,256]{0,2,1:T(8,128)(2,1)S(1)}, bf16[256,2,256]{0,2,1:T(8,128)(2,1)}, u32[]{:S(2)}) copy-start(bf16[256,2,256]{0,2,1:T(8,128)(2,1)} %copy.98) | copy-start | bytes 786436
  112.6 25.8 %copy-start.12 = (f32[256]{0:T(256)S(1)}, f32[256]{0:T(256)}, u32[]{:S(2)}) copy-start(f32[256]{0:T(256)} %param.21) | copy-start | bytes 3076
  116.2 17.3 %all-to-all-start.4 = ((s32[32,1,4]{2,1,0:T(1,128)}), s32[32,1,4]{2,1,0:T(1,128)S(1)}, u32[]{:S(2)}, u32[]{:S(2)}) async-start(s32[32,1,4]{2,1,0:T(1,128)} %bitcast.53), calls=%async_computation.4 | async-start | bytes 32768 | tf_op jit(solution)/shard_map/all_to_all | solution.py:145
  133.5 26.3 %all-to-all-start.3 = ((bf16[32,1,128,128]{3,2,1,0:T(8,128)(2,1)}), bf16[32,1,128,128]{3,2,1,0:T(8,128)(2,1)}, u32[]{:S(2)}, u32[]{:S(2)}) async-start(bf16[32,1,128,128]{3,2,1,0:T(8,128)(2,1)} %bitcast.140), calls=%async_computation.3 | async-start | bytes 2097152 | tf_op jit(solution)/shard_map/all_to_all | solution.py:143
  138.2 76.2 %all-reduce.3.cloned.1.call-start = ((), (), s32[]{:S(2)}) async-start(), calls=%async_computation.6 | async-start | bytes 2097152 | tf_op jit(solution)/shard_map/psum | solution.py:105
  140.6 3.2 copy-start.7
  140.6 3.2 copy-start.10
  147.2 68.6 %copy-start.5 = (bf16[256,2,128]{2,1,0:T(2,128)(2,1)S(1)}, bf16[256,2,128]{2,1,0:T(2,128)(2,1)}, u32[]{:S(2)}) copy-start(bf16[256,2,128]{2,1,0:T(2,128)(2,1)} %param.25) | copy-start | bytes 393220
  271.3 37.5 %copy-start.8 = (bf16[2,64,256]{2,1,0:T(8,128)(2,1)S(1)}, bf16[2,64,256]{2,1,0:T(8,128)(2,1)}, u32[]{:S(2)}) copy-start(bf16[2,64,256]{2,1,0:T(8,128)(2,1)} %param.31) | copy-start | bytes 196612
  273.6 102.8 %copy-start.3 = (bf16[512,256]{1,0:T(8,128)(2,1)S(1)}, bf16[512,256]{1,0:T(8,128)(2,1)}, u32[]{:S(2)}) copy-start(bf16[512,256]{1,0:T(8,128)(2,1)} %param.26) | copy-start | bytes 786436
  273.6 102.8 %copy-start.11 = (bf16[256,128]{1,0:T(8,128)(2,1)S(1)}, bf16[256,128]{1,0:T(8,128)(2,1)}, u32[]{:S(2)}) copy-start(bf16[256,128]{1,0:T(8,128)(2,1)} %param.32) | copy-start | bytes 196612
  273.6 102.8 %copy-start.13 = (bf16[128]{0:T(256)(128)(2,1)S(1)}, bf16[128]{0:T(256)(128)(2,1)}, u32[]{:S(2)}) copy-start(bf16[128]{0:T(256)(128)(2,1)} %param.33) | copy-start | bytes 772
  273.6 33.2 %all-to-all-start.5 = ((bf16[32,1,128,128]{3,2,1,0:T(8,128)(2,1)}), bf16[32,1,128,128]{3,2,1,0:T(8,128)(2,1)}, u32[]{:S(2)}, u32[]{:S(2)}) async-start(bf16[32,1,128,128]{3,2,1,0:T(8,128)(2,1)} %copy.108), calls=%async_computation.5 | async-start | bytes 2097152 | tf_op jit(solution)/shard_map/all_to_all | solution.py:176
  283.5 92.9 %all-reduce.5.cloned.1.call-start = ((), (), s32[]{:S(2)}) async-start(), calls=%async_computation.7 | async-start | bytes 1048576 | tf_op jit(solution)/shard_map/psum | solution.py:182
Sparse Core Ops, SparseCore 0:
  146.4 67.8 all-reduce.2
  310.0 66.3 all-reduce.4
where the time goes:
time: 401 us; the launch traced here: 400 us
  waiting for transfers between devices  179 us (45%)
  local copies, waits for them, and re-layouts  56.7 us (14%)
  blocking collectives  55.3 us (14%)
  starting transfers between devices  35.9 us (9%)
  matrix products  29.4 us (7%)
  other arithmetic  28.8 us (7%)
  between operations  14.4 us (4%)
    psum x1, waiting for transfers between devices, body(): cross_total = lax.psum(partial_cross, 'tensor')  65.9 us
    psum x1, waiting for transfers between devices, body(): head_total = lax.psum(partial_out, 'tensor')  52.2 us
    gather x8, local copies, waits for them, and re-layouts, one_group(): selected = jnp.take(cross_kv, member_group, axis=0)  24.4 us
    all_to_all x1, waiting for transfers between devices, body(): lax.all_to_all(answered, 'table', split_axis=0, concat_axis=0, tiled=True)  23.2 us
    all_to_all x1, blocking collectives, fetch_rows(): lax.all_to_all(wanted, 'table', split_axis=0, concat_axis=0, tiled=True)  19 us
    dot_general x4, matrix products, one_group(): jnp.einsum('ghck,gkhd->gchd', weights, values_sel, preferred_element_type...  17.8 us
    all_to_all x1, waiting for transfers between devices, fetch_rows(): lax.all_to_all(looked_up, 'table', split_axis=0, concat_axis=0, tiled=True)  16 us
    psum x1, blocking collectives, body(): scores_out = lax.psum(partial_score, 'tensor')  15 us
  transfers between devices with their start and end apart: 7, of which 7 were waited for; matrix products, arithmetic and copies ran while one was open for 7% of the time, Pallas kernels for 0%

commit v1 on v0

v1 whole, which is shorter than its diff:
```python
import functools
import math

import jax
import jax.numpy as jnp
from jax import lax
from jax.experimental import pallas as pl
from jax.experimental.pallas import tpu as pltpu
from jax.sharding import PartitionSpec as P

MESH = pl.DeviceIdType.MESH
F32, BF, I32 = jnp.float32, jnp.bfloat16, jnp.int32
A_OUT, A_KV, A_CQ, A_CO, A_MLP, A_SCORE, A_NORM, A_STATE = range(8)
S_MSG, S_REPLY, S_CAND, S_SCORE = range(4)


def dot(a, b):
    return lax.dot_general(a, b, (((1,), (0,)), ((), ())), preferred_element_type=F32)


def dot_nt(a, b):
    return lax.dot_general(a, b, (((1,), (1,)), ((), ())), preferred_element_type=F32)


def iota(shape, axis):
    return lax.broadcasted_iota(I32, shape, axis)


def silu_of_double(half):
    return half + half * jnp.tanh(half)


def kernel(
    T,
    K,
    SLAB,
    CAP,
    group_s,
    member_s,
    mask_s,
    owner_ref,
    row_ref,
    lngain_ref,
    wproj_ref,
    ngain_ref,
    wckv_ref,
    cand_ref,
    wscore_ref,
    table_hbm,
    wout_hbm,
    wcq_hbm,
    wco_hbm,
    wmlp_hbm,
    states_ref,
    scores_ref,
    tab,
    msg,
    m1,
    rep,
    replies,
    csend,
    call,
    wperm,
    wo_all,
    wkv_all,
    wcq_all,
    wco_all,
    wm_all,
    ws_all,
    hist_scr,
    nall,
    pg,
    pv,
    pq,
    pk,
    gs,
    gall,
    sall,
    q2,
    k2,
    v2,
    mb,
    um,
    cr,
    sr,
    rr,
    sc,
    lsem,
    tsend,
    trecv,
    asend,
    arecv,
    gsend,
    grecv,
    fsend,
    frecv,
):
    t, k = lax.axis_index("table"), lax.axis_index("tensor")
    X = K // 2
    x, core = k // 2, k % 2
    sib = k + 1 - 2 * core
    HIST = 64 * K
    R = T * 16
    CB = 16 * K
    NT = R // min(R, 128)
    TR = min(R, 128)
    SHIFT = SLAB.bit_length() - 1

    def local(i, src, dst):
        return pltpu.make_async_copy(src, dst, lsem.at[i])

    locals_ = [
        local(0, table_hbm, tab),
        local(1, wout_hbm, wo_all.at[k]),
        local(2, wcq_hbm, wcq_all.at[k]),
        local(3, wco_hbm, wco_all.at[k]),
        local(4, wmlp_hbm, wm_all.at[k]),
    ]
    for c in locals_:
        c.start()

    barrier = pltpu.get_barrier_semaphore()

    def greet(d, carry):
        pl.semaphore_signal(barrier, inc=1, device_id=(lax.rem(t + d, T), k), device_id_type=MESH)
        return carry

    lax.fori_loop(1, T, greet, 0)
    for d in range(1, K):
        pl.semaphore_signal(barrier, inc=1, device_id=(t, lax.rem(k + d, K)), device_id_type=MESH)

    def over_table(stage, src_of, buf):
        def one(d, carry):
            peer = lax.rem(t + d, T)
            pltpu.make_async_remote_copy(
                src_ref=src_of(peer),
                dst_ref=buf.at[t],
                send_sem=tsend.at[stage, peer],
                recv_sem=trecv.at[stage, t],
                device_id=(peer, k),
                device_id_type=MESH,
            ).start()
            return carry

        lax.fori_loop(1, T, one, 0)

    def table_wait(stage, buf, sends):
        def one(d, carry):
            peer = lax.rem(t + T - d, T)
            copy = pltpu.make_async_remote_copy(
                src_ref=buf.at[peer],
                dst_ref=buf.at[peer],
                send_sem=tsend.at[stage, peer],
                recv_sem=trecv.at[stage, peer],
                device_id=(peer, k),
                device_id_type=MESH,
            )
            if sends:
                copy.wait_send()
            else:
                copy.wait_recv()
            return carry

        lax.fori_loop(1, T, one, 0)

    order = sorted(range(1, X), key=lambda d: min(d, X - d))

    def gather_copy(a, src, buf, chunk, slot, dest):
        return pltpu.make_async_remote_copy(
            src_ref=src,
            dst_ref=buf.at[chunk],
            send_sem=asend.at[a, slot],
            recv_sem=arecv.at[a, chunk],
            device_id=(t, dest),
            device_id_type=MESH,
        )

    def gather_start(a, src, buf):
        for n, d in enumerate(order):
            gather_copy(a, src, buf, k, n, lax.rem(x + d, X) * 2 + core).start()
        gather_copy(a, src, buf, k, X - 1, sib).start()

    def gather_recv(a, buf, chunk):
        gather_copy(a, buf.at[chunk], buf, chunk, 0, sib).wait_recv()

    def near(n):
        return lax.rem(x + X - order[n], X) * 2 + core

    def far(n):
        return lax.rem(x + X - order[n], X) * 2 + 1 - core

    def gather_pass(a, buf, n):
        chunk = near(n)
        gather_recv(a, buf, chunk)
        gather_copy(a, buf.at[chunk], buf, chunk, X + n, sib).start()

    def gather_pass_all(a, buf):
        for n in range(X - 1):
            gather_pass(a, buf, n)

    def gather_rest(a, buf):
        gather_recv(a, buf, sib)
        for n in range(X - 1):
            gather_recv(a, buf, far(n))

    def gather_drain(a, buf):
        for slot in range(2 * X - 1):
            gather_copy(a, buf.at[k], buf, k, slot, sib).wait_send()

    ids = owner_ref[...] * SLAB + row_ref[...]
    own_row = jnp.concatenate([ids[0:1], ids[1:2]], axis=1)
    lane1 = iota((1, 128), 1)
    meta = jnp.zeros((1, 128), I32)
    for b in range(4):
        meta = jnp.where(lane1 == b, group_s[b], meta)
        meta = jnp.where(lane1 == 4 + b, member_s[b], meta)
        for q in range(4):
            meta = jnp.where(lane1 == 8 + 4 * b + q, mask_s[b, q], meta)
    msg[0:1, :] = own_row
    msg[1:2, :] = meta
    m1[t] = msg[...]

    pl.semaphore_wait(barrier, T - 1 + K - 1)
    over_table(S_MSG, lambda peer: msg, m1)

    gather_start(A_OUT, wout_hbm, wo_all)
    wckv = wckv_ref[...]
    kv0, kv1 = wckv[:, 0, :], wckv[:, 1, :]
    wkv_all[k] = jnp.concatenate([kv0[:, :64], kv1[:, :64], kv0[:, 64:], kv1[:, 64:]], axis=1)
    gather_start(A_KV, wkv_all.at[k], wkv_all)
    wproj = wproj_ref[...]
    w0, w1 = wproj[:, 0, :], wproj[:, 1, :]
    half_w = [w[:, 64 * i : 64 * i + 64] for i in range(4) for w in (w0, w1)]
    wperm[...] = jnp.concatenate(half_w, axis=1) * 0.5
    ws_all[k] = jnp.broadcast_to(wscore_ref[...].astype(F32).reshape(1, 128), (8, 128))

    upper = (iota((128, 128), 0) < iota((128, 128), 1)).astype(BF)
    own_slab = own_row >> SHIFT
    hot = iota((T, 128), 0) == own_slab
    rank = dot(hot.astype(BF), upper)
    slot_row = jnp.sum(jnp.where(hot, rank, 0.0), axis=0, keepdims=True) + own_slab.astype(F32) * (2 * CAP)
    eye = iota((128, 128), 0) == iota((128, 128), 1)
    slot_col = jnp.sum(jnp.where(eye, slot_row, 0.0), axis=1, keepdims=True).astype(I32)
    spots = iota((128, 2 * CAP * T), 1)
    pick_left = (spots == slot_col).astype(BF)
    pick_right = (spots == slot_col + CAP).astype(BF)

    table_wait(S_MSG, m1, False)
    wanted_ids = m1[:, 0, :]
    mine = (wanted_ids >> SHIFT) == t
    rank_in = dot(mine.astype(BF), upper)
    low = (wanted_ids & (SLAB - 1)).astype(F32)
    lane_t = iota((T, 128), 1)
    want = jnp.zeros((T, 128), F32)
    for r in range(CAP):
        of_r = jnp.sum(jnp.where(mine & (rank_in == r), low, 0.0), axis=1, keepdims=True)
        want = jnp.where(lane_t == r, of_r, want)
    want_i = want.astype(I32)
    spread = (iota((T * CAP, T), 0) // CAP == iota((T * CAP, T), 1)).astype(BF)
    high = dot(spread, (want_i >> 6).astype(F32).astype(BF))
    lower = dot(spread, (want_i & 63).astype(F32).astype(BF))
    in_lane = iota((T * CAP, 128), 1) == iota((T * CAP, 128), 0) % CAP
    want_col = jnp.sum(jnp.where(in_lane, high * 64.0 + lower, 0.0), axis=1, keepdims=True).astype(I32)
    locals_[0].wait()
    CH = min(512, SLAB)
    rows = jnp.zeros((T * CAP, 256), F32)
    at = iota((T * CAP, CH), 1)
    for c in range(SLAB // CH):
        rows += dot((at == want_col - c * CH).astype(BF), tab[c * CH : (c + 1) * CH, :])
    left = rows[:, :128].reshape(T, CAP, 128)
    right = rows[:, 128:].reshape(T, CAP, 128)
    rep[...] = jnp.concatenate([left, right], axis=1).astype(BF)
    replies[t] = rep[t]
    over_table(S_REPLY, lambda peer: rep.at[peer], replies)

    mine_c = jnp.concatenate(
        [cand_ref[pl.ds(pl.multiple_of(b * CB + 16 * k, 16), 16), :] for b in range(4)], axis=0
    )
    row_c, col_c = iota((R, 64), 0), iota((R, 64), 1)
    col_group = jnp.zeros((R, 64), I32)
    for b in range(4):
        col_group = jnp.where((col_c >> 4) == b, group_s[b], col_group)
    pick_c = ((row_c >> 4) == col_group) & ((row_c & 15) == (col_c & 15))
    csend[...] = dot(pick_c.astype(BF), mine_c).astype(BF).reshape(T, 16, 256)
    call[t] = csend[t]
    over_table(S_CAND, lambda peer: csend.at[peer], call)

    metas = m1[:, 1, :].astype(F32)

    def meta_lane(n):
        return jnp.sum(jnp.where(lane_t == n, metas, 0.0), axis=1, keepdims=True)

    here = [(meta_lane(b) == t.astype(F32)).astype(F32) for b in range(4)]
    member = sum(here[b] * meta_lane(4 + b) for b in range(4))
    reads = [sum(here[b] * meta_lane(8 + 4 * b + q) for b in range(4)) for q in range(4)]
    by_row = (iota((R, T), 0) >> 4 == iota((R, T), 1)).astype(BF)
    um[...] = dot(by_row, jnp.broadcast_to(member, (T, 128)).astype(BF))
    part = iota((T, HIST), 1) // (HIST // 4)
    reads_wide = jnp.zeros((T, HIST), F32)
    for q in range(4):
        reads_wide = jnp.where(part == q, reads[q], reads_wide)
    mb[...] = dot(by_row, reads_wide.astype(BF)).astype(BF)

    table_wait(S_REPLY, replies, False)
    got = replies[...].reshape(T * 2 * CAP, 128)
    history = jnp.concatenate([dot(pick_left, got), dot(pick_right, got)], axis=1)
    hist_scr[...] = history
    centred = history - jnp.mean(history, axis=1, keepdims=True)
    spread_v = jnp.mean(centred * centred, axis=1, keepdims=True)
    nall[k] = (centred * lax.rsqrt(spread_v + 1e-5) * lngain_ref[...]).astype(BF)
    gather_start(A_NORM, nall.at[k], nall)

    def project(chunk):
        half = dot(nall[chunk], wperm[...])
        out = silu_of_double(half).astype(BF)
        place = pl.ds(pl.multiple_of(chunk * 64, 64), 64)
        for n, ref in enumerate((pg, pv, pq, pk)):
            for u in range(2):
                ref[u, place, :] = out[64 * u : 64 * u + 64, 128 * n : 128 * n + 128]

    project(k)
    gather_recv(A_NORM, nall, sib)
    project(sib)
    for n in range(X - 1):
        gather_pass(A_NORM, nall, n)
        project(near(n))
    for n in range(X - 1):
        gather_recv(A_NORM, nall, far(n))
        project(far(n))

    gather_pass_all(A_OUT, wo_all)
    gather_pass_all(A_KV, wkv_all)
    gather_start(A_CQ, wcq_hbm, wcq_all)

    lane = iota((128, 128), 1)
    first = lane < 64
    same_half = jnp.where((iota((128, 128), 0) < 64) == first, 1.0 / 64, 0.0).astype(BF)
    causal = (iota((256, 128), 0) & 127) >= iota((256, 128), 1)
    gain_row = jnp.concatenate([ngain_ref[0:1, :], ngain_ref[1:2, :]], axis=1)
    zero = jnp.zeros((128, 128), BF)

    def gated_copy(u, piece, source):
        return pltpu.make_async_remote_copy(
            src_ref=gs.at[u, piece],
            dst_ref=gall.at[u, source],
            send_sem=gsend.at[u, piece],
            recv_sem=grecv.at[u, source],
            device_id=(t, piece),
            device_id_type=MESH,
        )

    for u in range(2):
        for block in range(HIST // 128):
            start = block * 128
            queries = pq[u, start : start + 128, :] * 0.0625
            both = jnp.concatenate([jnp.where(first, queries, zero), jnp.where(first, zero, queries)], axis=0)
            half = dot_nt(both, pk[u, start : start + 128, :])
            weights = jnp.where(causal, silu_of_double(half), 0.0).astype(BF)
            total = dot(weights, pv[u, start : start + 128, :])
            if block:
                weights = silu_of_double(dot_nt(both, pk[u, :start, :])).astype(BF)
                total += dot(weights, pv[u, :start, :])
            attended = jnp.where(first, total[:128], total[128:])
            coarse = attended.astype(BF)
            fine = (attended - coarse.astype(F32)).astype(BF)
            off = attended - (dot(coarse, same_half) + dot(fine, same_half))
            spread_a = dot((off * off).astype(BF), same_half)
            gate = pg[u, start : start + 128, :].astype(F32)
            gated = (off * lax.rsqrt(spread_a + 1e-5) * gain_row * gate).astype(BF)
            gs[u, 2 * block] = gated[:64]
            gs[u, 2 * block + 1] = gated[64:]
        gall[u, k] = gs[u, k]
        for d in range(1, K):
            gated_copy(u, lax.rem(k + d, K), k).start()

    gather_pass_all(A_CQ, wcq_all)
    table_wait(S_CAND, call, False)
    gather_rest(A_CQ, wcq_all)
    locals_[2].wait()
    first_r = iota((TR, 128), 1) < 64
    zero_r = jnp.zeros((TR, 128), BF)

    def make_queries(j, carry):
        for tile in range(NT):
            cands = call[tile * (TR // 16) : (tile + 1) * (TR // 16)].reshape(TR, 256)
            queries = dot_nt(cands, wcq_all[j]).astype(BF) * 0.0625
            one = um[tile * TR : (tile + 1) * TR, :] > 0.5
            parts = (jnp.where(one, zero_r, queries), jnp.where(one, queries, zero_r))
            q2[j, tile, :TR, :] = jnp.concatenate([jnp.where(first_r, q, zero_r) for q in parts], axis=1)
            q2[j, tile, TR:, :] = jnp.concatenate([jnp.where(first_r, zero_r, q) for q in parts], axis=1)
        return carry

    lax.fori_loop(0, K, make_queries, 0)

    gather_rest(A_OUT, wo_all)
    locals_[1].wait()
    for u in range(2):
        for d in range(1, K):
            source = lax.rem(k + K - d, K)
            gated_copy(u, source, source).wait_recv()
    total = hist_scr[...]
    for m in range(X):
        pair = [jnp.concatenate([gall[u, 2 * m], gall[u, 2 * m + 1]], axis=1) for u in range(2)]
        total += dot(jnp.concatenate(pair, axis=0), wo_all[2 * m : 2 * m + 2].reshape(256, 256))
    states = total.astype(BF)
    sall[k] = states
    gather_start(A_STATE, sall.at[k], sall)
    states_ref[...] = states.reshape(2, 64, 256)
    gather_start(A_CO, wco_hbm, wco_all)
    gather_start(A_MLP, wmlp_hbm, wm_all)
    gather_start(A_SCORE, ws_all.at[k], ws_all)

    gather_rest(A_KV, wkv_all)

    def make_kv(chunk):
        place = pl.ds(pl.multiple_of(chunk * 64, 64), 64)
        rows_s = sall[chunk]
        for j in range(K):
            kv = dot(rows_s, wkv_all[j]).astype(BF)
            for u in range(2):
                k2[j, place, 128 * u : 128 * u + 128] = kv[64 * u : 64 * u + 64, :128]
                v2[j, place, 128 * u : 128 * u + 128] = kv[64 * u : 64 * u + 64, 128:]

    make_kv(k)
    gather_recv(A_STATE, sall, sib)
    make_kv(sib)
    for n in range(X - 1):
        gather_pass(A_STATE, sall, n)
        make_kv(near(n))
    for n in range(X - 1):
        gather_recv(A_STATE, sall, far(n))
        make_kv(far(n))

    gather_pass_all(A_CO, wco_all)
    gather_pass_all(A_MLP, wm_all)
    gather_pass_all(A_SCORE, ws_all)

    def cross_pair(j, carry):
        for tile in range(NT):
            reads_t = mb[tile * TR : (tile + 1) * TR, :]
            half = dot_nt(q2[j, tile], k2[j])
            weights = silu_of_double(half).astype(BF)
            weights = jnp.concatenate([weights[:TR] * reads_t, weights[TR:] * reads_t], axis=0)
            out = dot(weights, v2[j])
            one = um[tile * TR : (tile + 1) * TR, :] > 0.5
            top = jnp.where(one, out[:TR, 128:], out[:TR, :128])
            bottom = jnp.where(one, out[TR:, 128:], out[TR:, :128])
            got_c = jnp.where(first_r, top, bottom) * (1.0 / math.sqrt(HIST))
            cr[j, tile * TR : (tile + 1) * TR, :] = got_c.astype(BF)
        return carry

    lax.fori_loop(0, K, cross_pair, 0)

    gather_rest(A_CO, wco_all)
    gather_rest(A_MLP, wm_all)
    gather_rest(A_SCORE, ws_all)
    locals_[3].wait()
    locals_[4].wait()
    mixed = call[...].reshape(R, 256).astype(F32)
    for m in range(X):
        pair = jnp.concatenate([cr[2 * m], cr[2 * m + 1]], axis=1)
        mixed += dot(pair, wco_all[2 * m : 2 * m + 2].reshape(256, 256))
    mixed = mixed.astype(BF)
    total_s = jnp.zeros((R, 128), F32)
    for m in range(X):
        half = dot(mixed, jnp.concatenate([wm_all[2 * m], wm_all[2 * m + 1]], axis=1)) * 0.5
        hidden = silu_of_double(half).astype(BF).astype(F32)
        total_s += hidden[:, :128] * ws_all[2 * m][0:1, :] + hidden[:, 128:] * ws_all[2 * m + 1][0:1, :]
    score = jnp.sum(total_s, axis=1, keepdims=True)
    at_lane = (iota((R, 128), 0) & 15) == (iota((R, 128), 1) & 15)
    by_slot = jnp.sum(jnp.where(at_lane, score, 0.0).reshape(T, 16, 128), axis=1)
    sr[...] = by_slot.reshape(T, 1, 128)
    rr[t] = sr[t]
    over_table(S_SCORE, lambda peer: sr.at[peer], rr)
    table_wait(S_SCORE, rr, False)
    back = rr[...].reshape(T, 128)
    groups = iota((T, 128), 0)
    own_lanes = (lane1 >> 4) == k
    blocks = [jnp.sum(jnp.where(groups == group_s[b], back, 0.0), axis=0, keepdims=True) for b in range(4)]
    sc[k] = jnp.where(own_lanes, jnp.concatenate(blocks, axis=0), 0.0)

    def score_copy(dest, source, slot):
        return pltpu.make_async_remote_copy(
            src_ref=sc.at[source],
            dst_ref=sc.at[source],
            send_sem=fsend.at[slot],
            recv_sem=frecv.at[source],
            device_id=(t, dest),
            device_id_type=MESH,
        )

    for d in range(1, K):
        score_copy(lax.rem(k + d, K), k, d).start()

    table_wait(S_MSG, m1, True)
    table_wait(S_REPLY, replies, True)
    table_wait(S_CAND, call, True)
    table_wait(S_SCORE, rr, True)
    for a, buf in (
        (A_OUT, wo_all),
        (A_KV, wkv_all),
        (A_CQ, wcq_all),
        (A_CO, wco_all),
        (A_MLP, wm_all),
        (A_SCORE, ws_all),
        (A_NORM, nall),
        (A_STATE, sall),
    ):
        gather_drain(a, buf)
    for u in range(2):
        for d in range(1, K):
            gated_copy(u, lax.rem(k + d, K), k).wait_send()
    for d in range(1, K):
        score_copy(lax.rem(k + d, K), k, d).wait_send()
    for d in range(1, K):
        source = lax.rem(k + K - d, K)
        score_copy(source, source, d).wait_recv()
    final = sc[0]
    for n in range(1, K):
        final += sc[n]
    scores_ref[...] = final


def body(
    T,
    K,
    table_rows,
    hist_owner,
    hist_row,
    ln_gain,
    w_proj,
    norm_gain,
    w_out,
    w_ckv,
    candidates,
    cand_group,
    cand_member,
    block_mask,
    w_cq,
    w_co,
    w_mlp,
    w_score,
):
    slab = table_rows.shape[0]
    cap = max(1, 2 * hist_owner.size // T)
    rows, hist = 16 * T, 64 * K
    tile = min(rows, 128)
    vmem, smem, anyspace = (
        pl.BlockSpec(memory_space=pltpu.VMEM),
        pl.BlockSpec(memory_space=pltpu.SMEM),
        pl.BlockSpec(memory_space=pl.ANY),
    )
    scratch = [
        pltpu.VMEM((slab, 256), BF),
        pltpu.VMEM((2, 128), I32),
        pltpu.VMEM((T, 2, 128), I32),
        pltpu.VMEM((T, 2 * cap, 128), BF),
        pltpu.VMEM((T, 2 * cap, 128), BF),
        pltpu.VMEM((T, 16, 256), BF),
        pltpu.VMEM((T, 16, 256), BF),
        pltpu.VMEM((256, 512), BF),
        pltpu.VMEM((K, 128, 256), BF),
        pltpu.VMEM((K, 256, 256), BF),
        pltpu.VMEM((K, 128, 256), BF),
        pltpu.VMEM((K, 128, 256), BF),
        pltpu.VMEM((K, 256, 128), BF),
        pltpu.VMEM((K, 8, 128), F32),
        pltpu.VMEM((128, 256), F32),
        pltpu.VMEM((K, 128, 256), BF),
        pltpu.VMEM((2, hist, 128), BF),
        pltpu.VMEM((2, hist, 128), BF),
        pltpu.VMEM((2, hist, 128), BF),
        pltpu.VMEM((2, hist, 128), BF),
        pltpu.VMEM((2, K, 64, 128), BF),
        pltpu.VMEM((2, K, 64, 128), BF),
        pltpu.VMEM((K, 128, 256), BF),
        pltpu.VMEM((K, rows // tile, 2 * tile, 256), BF),
        pltpu.VMEM((K, hist, 256), BF),
        pltpu.VMEM((K, hist, 256), BF),
        pltpu.VMEM((rows, hist), BF),
        pltpu.VMEM((rows, 128), F32),
        pltpu.VMEM((K, rows, 128), BF),
        pltpu.VMEM((T, 1, 128), F32),
        pltpu.VMEM((T, 1, 128), F32),
        pltpu.VMEM((K, 4, 128), F32),
        pltpu.SemaphoreType.DMA((5,)),
        pltpu.SemaphoreType.DMA((4, T)),
        pltpu.SemaphoreType.DMA((4, T)),
        pltpu.SemaphoreType.DMA((8, K)),
        pltpu.SemaphoreType.DMA((8, K)),
        pltpu.SemaphoreType.DMA((2, K)),
        pltpu.SemaphoreType.DMA((2, K)),
        pltpu.SemaphoreType.DMA((K,)),
        pltpu.SemaphoreType.DMA((K,)),
    ]
    states, scores = pl.pallas_call(
        functools.partial(kernel, T, K, slab, cap),
        out_shape=(
            jax.ShapeDtypeStruct((2, 64, 256), BF),
            jax.ShapeDtypeStruct((4, 128), F32),
        ),
        in_specs=[smem] * 3 + [vmem] * 8 + [anyspace] * 5,
        out_specs=(vmem, vmem),
        scratch_shapes=scratch,
        compiler_params=pltpu.CompilerParams(
            collective_id=0, has_side_effects=True, vmem_limit_bytes=48 * 1024 * 1024
        ),
    )(
        cand_group,
        cand_member,
        block_mask,
        hist_owner,
        hist_row,
        ln_gain.reshape(1, 256),
        w_proj,
        norm_gain,
        w_ckv,
        candidates,
        w_score.reshape(1, 128),
        table_rows,
        w_out.reshape(128, 256),
        jnp.transpose(w_cq, (1, 2, 0)).reshape(128, 256),
        w_co.reshape(128, 256),
        w_mlp,
    )
    return states, scores[:, : 16 * K].reshape(4 * 16 * K)


def solution(mesh):
    T, K = mesh.shape["table"], mesh.shape["tensor"]
    return jax.shard_map(
        functools.partial(body, T, K),
        mesh=mesh,
        in_specs=(
            P("table", None),
            P("table", "tensor"),
            P("table", "tensor"),
            P(),
            P(None, "tensor", None),
            P("tensor", None),
            P("tensor", None, None),
            P(None, "tensor", None),
            P("table", None),
            P("table"),
            P("table"),
            P("table", None),
            P(None, "tensor", None),
            P("tensor", None, None),
            P(None, "tensor"),
            P("tensor"),
        ),
        out_specs=(P("table", "tensor", None), P("table")),
        check_vma=False,
    )
```

time: 401 us -> 91.3 us (0.23)
  waiting for transfers between devices: 179 us -> 0 us
  Pallas kernels: 0 us -> 75.8 us
  blocking collectives: 55.3 us -> 0 us
  local copies, waits for them, and re-layouts: 56.7 us -> 14.3 us
  starting transfers between devices: 35.9 us -> 0 us
  matrix products: 29.4 us -> 0 us
  other arithmetic: 28.8 us -> 0 us
  between operations: 14.4 us -> 0.67 us
    psum x2 -> x0, waiting for transfers between devices: 118 us -> none  [the longest x1 65.9 us: body(): cross_total = lax.psum(partial_cross, 'tensor')]
    pallas_call x0 -> x1, Pallas kernels: none -> 75.8 us  [body(): pl.pallas_call(functools.partial(kernel, T, K, slab, cap), out_shape=(jax...]
    all_to_all x5 -> x0, waiting for transfers between devices: 61 us -> none  [the longest x1 23.2 us: body(): lax.all_to_all(answered, 'table', split_axis=0, concat_axis=0, tiled=True)]
    gather x13 -> x0, local copies, waits for them, and re-layouts: 38.8 us -> none  [the longest x8 24.4 us: one_group(): selected = jnp.take(cross_kv, member_group, axis=0)]
    all_to_all x5 -> x0, starting transfers between devices: 35.6 us -> none  [the longest x1 9.84 us: body(): lax.all_to_all(answered, 'table', split_axis=0, concat_axis=0, tiled=True)]
    dot_general x10 -> x0, matrix products: 28.3 us -> none  [the longest x4 17.8 us: one_group(): jnp.einsum('ghck,gkhd->gchd', weights, values_sel, preferred_element_type...]
    all_gather x2 -> x0, blocking collectives: 21.3 us -> none  [the longest x1 12.2 us: body(): lax.all_gather(hist_owner, 'tensor', axis=1, tiled=True)]
    all_to_all x1 -> x0, blocking collectives: 19 us -> none  [fetch_rows(): lax.all_to_all(wanted, 'table', split_axis=0, concat_axis=0, tiled=True)]
  transfers between devices with their start and end apart: 7 -> 0, of which waited for: 7 -> 0; matrix products, arithmetic and copies ran while one was open for 7% -> 0% of each run, Pallas kernels for 0% -> 0%
where the time goes in v1:
time: 91.3 us; the launch traced here: 90.8 us
  Pallas kernels  75.8 us (83%)
  local copies, waits for them, and re-layouts  14.3 us (16%)
    pallas_call x1, Pallas kernels, body(): pl.pallas_call(functools.partial(kernel, T, K, slab, cap), out_shape=(jax...  75.8 us
    unnamed x34, local copies, waits for them, and re-layouts  14.3 us

profile of v1, /device:TPU:1, one launch (start us, length us, event | category | flops | bytes accessed | tf_op | source)
XLA Modules:
  0.0 90.8 jit_solution(18397972837158870284)
XLA Ops:
  0.6 0.0 copy-start
  0.6 1.6 %copy-done = bf16[4096,256]{1,0:T(8,128)(2,1)S(1)} copy-done((bf16[4096,256]{1,0:T(8,128)(2,1)S(1)}, bf16[4096,256]{1,0:T(8,128)(2,1)}, u32[]{:S(2)}) %copy-start) | copy-done | bytes 2097176
  2.2 0.0 copy-start.1
  2.2 0.9 %copy-done.1 = bf16[256,2,256]{2,1,0:T(2,128)(2,1)S(1)} copy-done((bf16[256,2,256]{2,1,0:T(2,128)(2,1)S(1)}, bf16[256,2,256]{2,1,0:T(2,128)(2,1)}, u32[]{:S(2)}) %copy-start.1) | copy-done | bytes 262168
  3.2 0.0 copy-start.2
  3.2 0.9 %copy-done.2 = bf16[512,256]{1,0:T(8,128)(2,1)S(1)} copy-done((bf16[512,256]{1,0:T(8,128)(2,1)S(1)}, bf16[512,256]{1,0:T(8,128)(2,1)}, u32[]{:S(2)}) %copy-start.2) | copy-done | bytes 262168
  4.1 0.0 copy-start.3
  4.1 0.9 copy-done.3
  5.0 0.0 copy-start.4
  5.0 0.8 copy-done.4
  5.9 0.0 copy-start.5
  5.9 0.8 copy-done.5
  6.7 0.0 copy-start.6
  6.7 0.8 copy-done.6
  7.6 0.0 copy-start.7
  7.6 0.8 copy-done.7
  8.4 0.0 copy-start.8
  8.4 0.7 copy-done.8
  9.1 0.0 copy-start.9
  9.1 0.7 copy-done.9
  9.8 0.0 copy-start.10
  9.8 0.7 copy-done.10
  10.4 0.0 copy-start.11
  10.4 0.7 copy-done.11
  11.1 0.0 copy-start.12
  11.1 0.7 copy-done.12
  11.8 0.0 copy-start.13
  11.8 0.7 copy-done.13
  12.5 0.0 copy-start.14
  12.5 0.7 copy-done.14
  13.1 0.0 copy-start.15
  13.1 0.7 copy-done.15
  13.8 75.8 %shard_map.167 = (bf16[2,64,256]{2,1,0:T(8,128)(2,1)S(1)}, f32[4,128]{1,0:T(4,128)S(1)}) custom-call(s32[4]{0:T(128)S(1)} %copy-done.13, s32[4]{0:T(128)S(1)} %copy-done.14, s32[4,4]{1,0:T(4,128)S(1)} %copy-done.8, s32[2,64]{1,0:T(2,128)S(1)} %copy-done.9, s32[2,64]{1,0:T(2,128)S(1)} %copy-done.10, f32[1,256]{1,0:T(1,128)S(1)} %bitcast.12, ...), custom_call_target="tpu_custom_call" | custom-call | tf_op jit(solution)/shard_map/pallas_call | solution.py:596
  89.6 0.6 copy.20
  90.2 0.6 copy.21
Async XLA Ops:
  0.6 1.6 %copy-start = (bf16[4096,256]{1,0:T(8,128)(2,1)S(1)}, bf16[4096,256]{1,0:T(8,128)(2,1)}, u32[]{:S(2)}) copy-start(bf16[4096,256]{1,0:T(8,128)(2,1)} %table_hbm.1) | copy-start | bytes 6291460
  2.2 0.9 %copy-start.1 = (bf16[256,2,256]{2,1,0:T(2,128)(2,1)S(1)}, bf16[256,2,256]{2,1,0:T(2,128)(2,1)}, u32[]{:S(2)}) copy-start(bf16[256,2,256]{2,1,0:T(2,128)(2,1)} %wproj_ref.1) | copy-start | bytes 786436
  3.2 0.9 %copy-start.2 = (bf16[512,256]{1,0:T(8,128)(2,1)S(1)}, bf16[512,256]{1,0:T(8,128)(2,1)}, u32[]{:S(2)}) copy-start(bf16[512,256]{1,0:T(8,128)(2,1)} %cand_ref.1) | copy-start | bytes 786436
  4.1 0.9 copy-start.3
  5.0 0.8 copy-start.4
  5.9 0.8 copy-start.5
  6.7 0.8 copy-start.6
  7.6 0.8 copy-start.7
  8.4 0.7 copy-start.8
  9.1 0.7 copy-start.9
  9.8 0.7 copy-start.10
  10.4 0.7 copy-start.11
  11.1 0.7 copy-start.12
  11.8 0.7 copy-start.13
  12.5 0.7 copy-start.14
  13.1 0.7 copy-start.15

commit v2 on v1

--- a/solution.py
+++ b/solution.py
@@ -35,6 +35,24 @@
     K,
     SLAB,
     CAP,
+    group_hbm,
+    member_hbm,
+    mask_hbm,
+    owner_hbm,
+    row_hbm,
+    lngain_hbm,
+    wproj_hbm,
+    ngain_hbm,
+    wckv_hbm,
+    cand_hbm,
+    wscore_hbm,
+    table_hbm,
+    wout_hbm,
+    wcq_hbm,
+    wco_hbm,
+    wmlp_hbm,
+    states_ref,
+    scores_ref,
     group_s,
     member_s,
     mask_s,
@@ -46,13 +64,6 @@
     wckv_ref,
     cand_ref,
     wscore_ref,
-    table_hbm,
-    wout_hbm,
-    wcq_hbm,
-    wco_hbm,
-    wmlp_hbm,
-    states_ref,
-    scores_ref,
     tab,
     msg,
     m1,
@@ -116,7 +127,24 @@
         local(3, wco_hbm, wco_all.at[k]),
         local(4, wmlp_hbm, wm_all.at[k]),
     ]
-    for c in locals_:
+    ids_in = [
+        local(5, owner_hbm, owner_ref),
+        local(6, row_hbm, row_ref),
+        local(7, group_hbm, group_s),
+        local(8, member_hbm, member_s),
+        local(9, mask_hbm, mask_s),
+    ]
+    weights_in = [
+        local(10, wckv_hbm, wckv_ref),
+        local(11, wproj_hbm, wproj_ref),
+        local(12, wscore_hbm, wscore_ref),
+    ]
+    late_in = [
+        local(13, cand_hbm, cand_ref),
+        local(14, lngain_hbm, lngain_ref),
+        local(15, ngain_hbm, ngain_ref),
+    ]
+    for c in ids_in + weights_in + locals_ + late_in:
         c.start()
 
     barrier = pltpu.get_barrier_semaphore()
@@ -207,6 +235,8 @@
         for slot in range(2 * X - 1):
             gather_copy(a, buf.at[k], buf, k, slot, sib).wait_send()
 
+    for c in ids_in:
+        c.wait()
     ids = owner_ref[...] * SLAB + row_ref[...]
     own_row = jnp.concatenate([ids[0:1], ids[1:2]], axis=1)
     lane1 = iota((1, 128), 1)
@@ -224,6 +254,8 @@
     over_table(S_MSG, lambda peer: msg, m1)
 
     gather_start(A_OUT, wout_hbm, wo_all)
+    for c in weights_in:
+        c.wait()
     wckv = wckv_ref[...]
     kv0, kv1 = wckv[:, 0, :], wckv[:, 1, :]
     wkv_all[k] = jnp.concatenate([kv0[:, :64], kv1[:, :64], kv0[:, 64:], kv1[:, 64:]], axis=1)
@@ -273,6 +305,8 @@
     replies[t] = rep[t]
     over_table(S_REPLY, lambda peer: rep.at[peer], replies)
 
+    for c in late_in:
+        c.wait()
     mine_c = jnp.concatenate(
         [cand_ref[pl.ds(pl.multiple_of(b * CB + 16 * k, 16), 16), :] for b in range(4)], axis=0
     )
@@ -545,12 +579,19 @@
     cap = max(1, 2 * hist_owner.size // T)
     rows, hist = 16 * T, 64 * K
     tile = min(rows, 128)
-    vmem, smem, anyspace = (
-        pl.BlockSpec(memory_space=pltpu.VMEM),
-        pl.BlockSpec(memory_space=pltpu.SMEM),
-        pl.BlockSpec(memory_space=pl.ANY),
-    )
+    vmem, hbm = pl.BlockSpec(memory_space=pltpu.VMEM), pl.BlockSpec(memory_space=pltpu.HBM)
     scratch = [
+        pltpu.SMEM((4,), I32),
+        pltpu.SMEM((4,), I32),
+        pltpu.SMEM((4, 4), I32),
+        pltpu.VMEM((2, 64), I32),
+        pltpu.VMEM((2, 64), I32),
+        pltpu.VMEM((1, 256), F32),
+        pltpu.VMEM((256, 2, 256), BF),
+        pltpu.VMEM((2, 64), F32),
+        pltpu.VMEM((256, 2, 128), BF),
+        pltpu.VMEM((64 * K, 256), BF),
+        pltpu.VMEM((1, 128), BF),
         pltpu.VMEM((slab, 256), BF),
         pltpu.VMEM((2, 128), I32),
         pltpu.VMEM((T, 2, 128), I32),
@@ -583,7 +624,7 @@
         pltpu.VMEM((T, 1, 128), F32),
         pltpu.VMEM((T, 1, 128), F32),
         pltpu.VMEM((K, 4, 128), F32),
-        pltpu.SemaphoreType.DMA((5,)),
+        pltpu.SemaphoreType.DMA((16,)),
         pltpu.SemaphoreType.DMA((4, T)),
         pltpu.SemaphoreType.DMA((4, T)),
         pltpu.SemaphoreType.DMA((8, K)),
@@ -599,11 +640,11 @@
             jax.ShapeDtypeStruct((2, 64, 256), BF),
             jax.ShapeDtypeStruct((4, 128), F32),
         ),
-        in_specs=[smem] * 3 + [vmem] * 8 + [anyspace] * 5,
+        in_specs=[hbm] * 16,
         out_specs=(vmem, vmem),
         scratch_shapes=scratch,
         compiler_params=pltpu.CompilerParams(
-            collective_id=0, has_side_effects=True, vmem_limit_bytes=48 * 1024 * 1024
+            collective_id=0, has_side_effects=True, vmem_limit_bytes=60 * 1024 * 1024
         ),
     )(
         cand_group,

time: 91.3 us -> 79.4 us (0.87)
  local copies, waits for them, and re-layouts: 14.3 us -> 2.72 us
    unnamed x34 -> x2, local copies, waits for them, and re-layouts: 14.3 us -> 2.72 us
where the time goes in v2:
time: 79.4 us; the launch traced here: 79.2 us
  Pallas kernels  75.9 us (96%)
  local copies, waits for them, and re-layouts  2.72 us (3%)
    pallas_call x1, Pallas kernels, body(): pl.pallas_call(functools.partial(kernel, T, K, slab, cap), out_shape=(jax...  75.9 us
    unnamed x2, local copies, waits for them, and re-layouts  2.72 us

profile of v2, /device:TPU:1, one launch (start us, length us, event | category | flops | bytes accessed | tf_op | source)
XLA Modules:
  0.0 79.2 jit_solution(13138581419207009984)
XLA Ops:
  0.6 75.9 %shard_map.167 = (bf16[2,64,256]{2,1,0:T(8,128)(2,1)}, f32[4,128]{1,0:T(4,128)}) custom-call(s32[4]{0:T(128)} %group_hbm.1, s32[4]{0:T(128)} %member_hbm.1, s32[4,4]{1,0:T(4,128)} %mask_hbm.1, s32[2,64]{1,0:T(2,128)} %owner_hbm.1, s32[2,64]{1,0:T(2,128)} %row_hbm.1, f32[1,256]{1,0:T(1,128)} %bitcast.12, bf16[256,2,256]{2,1,0:T(2,128)(2,1)} %wproj_hbm.1, ...), custom_call_target="tpu_custom_call" | custom-call | tf_op jit(solution)/shard_map/pallas_call | solution.py:637
  76.5 1.5 %copy.20 = bf16[2,64,256]{2,1,0:T(8,128)(2,1)} copy(bf16[2,64,256]{2,1,0:T(8,128)(2,1)} %get-tuple-element.8) | data formatting | bytes 131072
  78.0 1.2 %copy.21 = f32[512]{0:T(512)} copy(f32[512]{0:T(512)} %bitcast.11) | data formatting | bytes 4096

commit v3 on v2

--- a/solution.py
+++ b/solution.py
@@ -10,7 +10,7 @@
 
 MESH = pl.DeviceIdType.MESH
 F32, BF, I32 = jnp.float32, jnp.bfloat16, jnp.int32
-A_OUT, A_KV, A_CQ, A_CO, A_MLP, A_SCORE, A_NORM, A_STATE = range(8)
+A_OUT, A_K, A_V, A_CQ, A_CO, A_MLP, A_SCORE, A_STATE = range(8)
 S_MSG, S_REPLY, S_CAND, S_SCORE = range(4)
 
 
@@ -72,13 +72,16 @@
     csend,
     call,
     wperm,
+    gains,
     wo_all,
-    wkv_all,
+    wk_all,
+    wv_all,
     wcq_all,
     wco_all,
     wm_all,
     ws_all,
     hist_scr,
+    nown,
     nall,
     pg,
     pv,
@@ -92,7 +95,6 @@
     v2,
     mb,
     um,
-    cr,
     sr,
     rr,
     sc,
@@ -101,6 +103,11 @@
     trecv,
     asend,
     arecv,
+    hrecv,
+    psend,
+    precv,
+    nsend,
+    nrecv,
     gsend,
     grecv,
     fsend,
@@ -113,8 +120,8 @@
     HIST = 64 * K
     R = T * 16
     CB = 16 * K
-    NT = R // min(R, 128)
-    TR = min(R, 128)
+    TR = min(R, 256)
+    NT = R // TR
     SHIFT = SLAB.bit_length() - 1
 
     def local(i, src, dst):
@@ -138,11 +145,11 @@
         local(10, wckv_hbm, wckv_ref),
         local(11, wproj_hbm, wproj_ref),
         local(12, wscore_hbm, wscore_ref),
+        local(15, ngain_hbm, ngain_ref),
     ]
     late_in = [
         local(13, cand_hbm, cand_ref),
         local(14, lngain_hbm, lngain_ref),
-        local(15, ngain_hbm, ngain_ref),
     ]
     for c in ids_in + weights_in + locals_ + late_in:
         c.start()
@@ -222,10 +229,6 @@
         gather_recv(a, buf, chunk)
         gather_copy(a, buf.at[chunk], buf, chunk, X + n, sib).start()
 
-    def gather_pass_all(a, buf):
-        for n in range(X - 1):
-            gather_pass(a, buf, n)
-
     def gather_rest(a, buf):
         gather_recv(a, buf, sib)
         for n in range(X - 1):
@@ -234,6 +237,56 @@
     def gather_drain(a, buf):
         for slot in range(2 * X - 1):
             gather_copy(a, buf.at[k], buf, k, slot, sib).wait_send()
+
+    assert X == 4
+    right, left = lax.rem(x + 1, X) * 2 + core, lax.rem(x + X - 1, X) * 2 + core
+    across = lax.rem(x + 2, X) * 2 + core
+
+    def half_copy(a, buf, chunk, side, dest):
+        size = buf.shape[1] // 2
+        part = buf.at[chunk, pl.ds(side * size, size)]
+        return pltpu.make_async_remote_copy(
+            src_ref=part,
+            dst_ref=part,
+            send_sem=asend.at[a, 3 + side],
+            recv_sem=hrecv.at[a, side],
+            device_id=(t, dest),
+            device_id_type=MESH,
+        )
+
+    def relay_start(a, src, buf):
+        gather_copy(a, src, buf, k, 0, right).start()
+        gather_copy(a, src, buf, k, 1, left).start()
+        gather_copy(a, src, buf, k, 2, sib).start()
+
+    def relay_pass(a, buf):
+        gather_recv(a, buf, left)
+        half_copy(a, buf, left, 0, right).start()
+        gather_copy(a, buf.at[left], buf, left, 5, sib).start()
+        gather_recv(a, buf, right)
+        half_copy(a, buf, right, 1, left).start()
+        gather_copy(a, buf.at[right], buf, right, 6, sib).start()
+
+    def relay_finish(a, buf):
+        half_copy(a, buf, across, 0, sib).wait_recv()
+        half_copy(a, buf, across, 1, sib).wait_recv()
+        gather_copy(a, buf.at[across], buf, across, 7, sib).start()
+
+    def relay_drain(a, buf):
+        for slot in (0, 1, 2, 5, 6, 7):
+            gather_copy(a, buf.at[k], buf, k, slot, sib).wait_send()
+        half_copy(a, buf, left, 0, right).wait_send()
+        half_copy(a, buf, right, 1, left).wait_send()
+
+    def pair_copy(n, buf, slot):
+        return pltpu.make_async_remote_copy(
+            src_ref=buf.at[slot],
+            dst_ref=buf.at[slot],
+            send_sem=psend.at[n],
+            recv_sem=precv.at[n],
+            device_id=(t, sib),
+            device_id_type=MESH,
+        )
 
     for c in ids_in:
         c.wait()
@@ -253,17 +306,22 @@
     pl.semaphore_wait(barrier, T - 1 + K - 1)
     over_table(S_MSG, lambda peer: msg, m1)
 
-    gather_start(A_OUT, wout_hbm, wo_all)
+    relay_start(A_OUT, wout_hbm, wo_all)
     for c in weights_in:
         c.wait()
     wckv = wckv_ref[...]
     kv0, kv1 = wckv[:, 0, :], wckv[:, 1, :]
-    wkv_all[k] = jnp.concatenate([kv0[:, :64], kv1[:, :64], kv0[:, 64:], kv1[:, 64:]], axis=1)
-    gather_start(A_KV, wkv_all.at[k], wkv_all)
+    wk_all[k] = jnp.concatenate([kv0[:, :64], kv1[:, :64]], axis=1).T
+    wv_all[k] = jnp.concatenate([kv0[:, 64:], kv1[:, 64:]], axis=1)
+    relay_start(A_K, wk_all.at[k], wk_all)
+    relay_start(A_V, wv_all.at[k], wv_all)
     wproj = wproj_ref[...]
     w0, w1 = wproj[:, 0, :], wproj[:, 1, :]
     half_w = [w[:, 64 * i : 64 * i + 64] for i in range(4) for w in (w0, w1)]
-    wperm[...] = jnp.concatenate(half_w, axis=1) * 0.5
+    wperm[core] = jnp.concatenate(half_w, axis=1) * 0.5
+    gains[core] = jnp.concatenate([ngain_ref[0:1, :], ngain_ref[1:2, :]], axis=1)
+    pair_copy(0, wperm, core).start()
+    pair_copy(1, gains, core).start()
     ws_all[k] = jnp.broadcast_to(wscore_ref[...].astype(F32).reshape(1, 128), (8, 128))
 
     upper = (iota((128, 128), 0) < iota((128, 128), 1)).astype(BF)
@@ -278,6 +336,10 @@
     pick_right = (spots == slot_col + CAP).astype(BF)
 
     table_wait(S_MSG, m1, False)
+    relay_start(A_CQ, wcq_hbm, wcq_all)
+    relay_start(A_CO, wco_hbm, wco_all)
+    relay_start(A_MLP, wmlp_hbm, wm_all)
+    gather_start(A_SCORE, ws_all.at[k], ws_all)
     wanted_ids = m1[:, 0, :]
     mine = (wanted_ids >> SHIFT) == t
     rank_in = dot(mine.astype(BF), upper)
@@ -299,11 +361,14 @@
     at = iota((T * CAP, CH), 1)
     for c in range(SLAB // CH):
         rows += dot((at == want_col - c * CH).astype(BF), tab[c * CH : (c + 1) * CH, :])
-    left = rows[:, :128].reshape(T, CAP, 128)
-    right = rows[:, 128:].reshape(T, CAP, 128)
-    rep[...] = jnp.concatenate([left, right], axis=1).astype(BF)
+    halves = [rows[:, :128].reshape(T, CAP, 128), rows[:, 128:].reshape(T, CAP, 128)]
+    rep[...] = jnp.concatenate(halves, axis=1).astype(BF)
     replies[t] = rep[t]
     over_table(S_REPLY, lambda peer: rep.at[peer], replies)
+
+    relay_pass(A_OUT, wo_all)
+    relay_pass(A_K, wk_all)
+    relay_pass(A_V, wv_all)
 
     for c in late_in:
         c.wait()
@@ -317,7 +382,6 @@
     pick_c = ((row_c >> 4) == col_group) & ((row_c & 15) == (col_c & 15))
     csend[...] = dot(pick_c.astype(BF), mine_c).astype(BF).reshape(T, 16, 256)
     call[t] = csend[t]
-    over_table(S_CAND, lambda peer: csend.at[peer], call)
 
     metas = m1[:, 1, :].astype(F32)
 
@@ -329,7 +393,7 @@
     reads = [sum(here[b] * meta_lane(8 + 4 * b + q) for b in range(4)) for q in range(4)]
     by_row = (iota((R, T), 0) >> 4 == iota((R, T), 1)).astype(BF)
     um[...] = dot(by_row, jnp.broadcast_to(member, (T, 128)).astype(BF))
-    part = iota((T, HIST), 1) // (HIST // 4)
+    part = (iota((T, HIST), 1) % (HIST // 2)) // (HIST // 8)
     reads_wide = jnp.zeros((T, HIST), F32)
     for q in range(4):
         reads_wide = jnp.where(part == q, reads[q], reads_wide)
@@ -341,73 +405,99 @@
     hist_scr[...] = history
     centred = history - jnp.mean(history, axis=1, keepdims=True)
     spread_v = jnp.mean(centred * centred, axis=1, keepdims=True)
-    nall[k] = (centred * lax.rsqrt(spread_v + 1e-5) * lngain_ref[...]).astype(BF)
-    gather_start(A_NORM, nall.at[k], nall)
-
-    def project(chunk):
-        half = dot(nall[chunk], wperm[...])
-        out = silu_of_double(half).astype(BF)
-        place = pl.ds(pl.multiple_of(chunk * 64, 64), 64)
-        for n, ref in enumerate((pg, pv, pq, pk)):
-            for u in range(2):
-                ref[u, place, :] = out[64 * u : 64 * u + 64, 128 * n : 128 * n + 128]
-
-    project(k)
-    gather_recv(A_NORM, nall, sib)
-    project(sib)
+    normed = (centred * lax.rsqrt(spread_v + 1e-5) * lngain_ref[...]).astype(BF)
+    nown[0] = normed[:64]
+    nown[1] = normed[64:]
+
+    def normed_copy(dest, source):
+        return pltpu.make_async_remote_copy(
+            src_ref=nown.at[dest % 2],
+            dst_ref=nall.at[source],
+            send_sem=nsend.at[dest],
+            recv_sem=nrecv.at[source],
+            device_id=(t, dest),
+            device_id_type=MESH,
+        )
+
+    def others(n):
+        return lax.rem(k + n, K)
+
+    for n in range(1, K):
+        normed_copy(others(n), k).start()
+    nall[k] = nown[core]
+    over_table(S_CAND, lambda peer: csend.at[peer], call)
+    pair_copy(0, wperm, 1 - core).wait_recv()
+    pair_copy(1, gains, 1 - core).wait_recv()
+
+    def project(chip):
+        rows_n = nall[pl.ds(2 * chip, 2)].reshape(128, 256)
+        place = pl.ds(pl.multiple_of(chip * 128, 128), 128)
+        for p in range(2):
+            out = silu_of_double(dot(rows_n, wperm[p])).astype(BF)
+            for n, ref in enumerate((pg, pv, pq, pk)):
+                ref[p, place, :] = out[:, 128 * n : 128 * n + 128]
+
+    normed_copy(sib, sib).wait_recv()
+    project(x)
+    for d in order:
+        chip = lax.rem(x + d, X)
+        for c in range(2):
+            normed_copy(2 * chip + c, 2 * chip + c).wait_recv()
+        project(chip)
+    relay_finish(A_OUT, wo_all)
+    relay_finish(A_K, wk_all)
+    relay_finish(A_V, wv_all)
+    relay_pass(A_CQ, wcq_all)
+    relay_pass(A_CO, wco_all)
+    relay_pass(A_MLP, wm_all)
     for n in range(X - 1):
-        gather_pass(A_NORM, nall, n)
-        project(near(n))
-    for n in range(X - 1):
-        gather_recv(A_NORM, nall, far(n))
-        project(far(n))
-
-    gather_pass_all(A_OUT, wo_all)
-    gather_pass_all(A_KV, wkv_all)
-    gather_start(A_CQ, wcq_hbm, wcq_all)
+        gather_pass(A_SCORE, ws_all, n)
 
     lane = iota((128, 128), 1)
     first = lane < 64
     same_half = jnp.where((iota((128, 128), 0) < 64) == first, 1.0 / 64, 0.0).astype(BF)
     causal = (iota((256, 128), 0) & 127) >= iota((256, 128), 1)
-    gain_row = jnp.concatenate([ngain_ref[0:1, :], ngain_ref[1:2, :]], axis=1)
     zero = jnp.zeros((128, 128), BF)
 
-    def gated_copy(u, piece, source):
+    def gated_copy(dest, source):
         return pltpu.make_async_remote_copy(
-            src_ref=gs.at[u, piece],
-            dst_ref=gall.at[u, source],
-            send_sem=gsend.at[u, piece],
-            recv_sem=grecv.at[u, source],
-            device_id=(t, piece),
+            src_ref=gs.at[dest],
+            dst_ref=gall.at[source % 2, source // 2],
+            send_sem=gsend.at[dest],
+            recv_sem=grecv.at[source],
+            device_id=(t, dest),
             device_id_type=MESH,
         )
 
-    for u in range(2):
-        for block in range(HIST // 128):
-            start = block * 128
-            queries = pq[u, start : start + 128, :] * 0.0625
+    for block in range(HIST // 128):
+        start = block * 128
+        for p in range(2):
+            queries = pq[p, start : start + 128, :] * 0.0625
             both = jnp.concatenate([jnp.where(first, queries, zero), jnp.where(first, zero, queries)], axis=0)
-            half = dot_nt(both, pk[u, start : start + 128, :])
+            half = dot_nt(both, pk[p, start : start + 128, :])
             weights = jnp.where(causal, silu_of_double(half), 0.0).astype(BF)
-            total = dot(weights, pv[u, start : start + 128, :])
+            total = dot(weights, pv[p, start : start + 128, :])
             if block:
-                weights = silu_of_double(dot_nt(both, pk[u, :start, :])).astype(BF)
-                total += dot(weights, pv[u, :start, :])
+                weights = silu_of_double(dot_nt(both, pk[p, :start, :])).astype(BF)
+                total += dot(weights, pv[p, :start, :])
             attended = jnp.where(first, total[:128], total[128:])
             coarse = attended.astype(BF)
             fine = (attended - coarse.astype(F32)).astype(BF)
             off = attended - (dot(coarse, same_half) + dot(fine, same_half))
             spread_a = dot((off * off).astype(BF), same_half)
-            gate = pg[u, start : start + 128, :].astype(F32)
-            gated = (off * lax.rsqrt(spread_a + 1e-5) * gain_row * gate).astype(BF)
-            gs[u, 2 * block] = gated[:64]
-            gs[u, 2 * block + 1] = gated[64:]
-        gall[u, k] = gs[u, k]
-        for d in range(1, K):
-            gated_copy(u, lax.rem(k + d, K), k).start()
-
-    gather_pass_all(A_CQ, wcq_all)
+            gate = pg[p, start : start + 128, :].astype(F32)
+            gated = (off * lax.rsqrt(spread_a + 1e-5) * gains[p] * gate).astype(BF)
+            gs[2 * block, :, 128 * p : 128 * p + 128] = gated[:64]
+            gs[2 * block + 1, :, 128 * p : 128 * p + 128] = gated[64:]
+        for dest in (2 * block, 2 * block + 1):
+
+            @pl.when(k != dest)
+            def _():
+                gated_copy(dest, k).start()
+
+    gall[core, x] = gs[k]
+
+    relay_finish(A_CQ, wcq_all)
     table_wait(S_CAND, call, False)
     gather_rest(A_CQ, wcq_all)
     locals_[2].wait()
@@ -424,88 +514,99 @@
             q2[j, tile, TR:, :] = jnp.concatenate([jnp.where(first_r, zero_r, q) for q in parts], axis=1)
         return carry
 
-    lax.fori_loop(0, K, make_queries, 0)
+    lax.fori_loop(0, K // 2, make_queries, 0)
 
     gather_rest(A_OUT, wo_all)
     locals_[1].wait()
-    for u in range(2):
-        for d in range(1, K):
-            source = lax.rem(k + K - d, K)
-            gated_copy(u, source, source).wait_recv()
+    for n in range(1, K):
+        gated_copy(others(n), others(n)).wait_recv()
     total = hist_scr[...]
     for m in range(X):
-        pair = [jnp.concatenate([gall[u, 2 * m], gall[u, 2 * m + 1]], axis=1) for u in range(2)]
-        total += dot(jnp.concatenate(pair, axis=0), wo_all[2 * m : 2 * m + 2].reshape(256, 256))
+        pieces = jnp.concatenate([gall[0, m], gall[1, m]], axis=0)
+        total += dot(pieces, wo_all[2 * m : 2 * m + 2].reshape(256, 256))
     states = total.astype(BF)
     sall[k] = states
     gather_start(A_STATE, sall.at[k], sall)
     states_ref[...] = states.reshape(2, 64, 256)
-    gather_start(A_CO, wco_hbm, wco_all)
-    gather_start(A_MLP, wmlp_hbm, wm_all)
-    gather_start(A_SCORE, ws_all.at[k], ws_all)
-
-    gather_rest(A_KV, wkv_all)
-
-    def make_kv(chunk):
-        place = pl.ds(pl.multiple_of(chunk * 64, 64), 64)
-        rows_s = sall[chunk]
-        for j in range(K):
-            kv = dot(rows_s, wkv_all[j]).astype(BF)
-            for u in range(2):
-                k2[j, place, 128 * u : 128 * u + 128] = kv[64 * u : 64 * u + 64, :128]
-                v2[j, place, 128 * u : 128 * u + 128] = kv[64 * u : 64 * u + 64, 128:]
-
-    make_kv(k)
-    gather_recv(A_STATE, sall, sib)
-    make_kv(sib)
+    relay_finish(A_CO, wco_all)
+    relay_finish(A_MLP, wm_all)
+
+    lax.fori_loop(K // 2, K, make_queries, 0)
+
+    gather_rest(A_K, wk_all)
+    gather_rest(A_V, wv_all)
+
+    def make_kv(part, own):
+        place = slice(part * (HIST // 2), (part + 1) * (HIST // 2))
+        values_w = jnp.concatenate([wv_all[j] for j in range(K)], axis=1)
+        for u in range(2):
+            rows_s = jnp.concatenate([sall[2 * m + own, 64 * u : 64 * u + 64, :] for m in range(X)], axis=0)
+            keys = dot_nt(wk_all[...].reshape(K * 128, 256), rows_s).astype(BF)
+            values = dot(rows_s, values_w).astype(BF)
+            for j in range(K):
+                k2[j, 128 * u : 128 * u + 128, place] = keys[128 * j : 128 * j + 128]
+                v2[j, place, 128 * u : 128 * u + 128] = values[:, 128 * j : 128 * j + 128]
+
     for n in range(X - 1):
         gather_pass(A_STATE, sall, n)
-        make_kv(near(n))
-    for n in range(X - 1):
-        gather_recv(A_STATE, sall, far(n))
-        make_kv(far(n))
-
-    gather_pass_all(A_CO, wco_all)
-    gather_pass_all(A_MLP, wm_all)
-    gather_pass_all(A_SCORE, ws_all)
-
-    def cross_pair(j, carry):
-        for tile in range(NT):
-            reads_t = mb[tile * TR : (tile + 1) * TR, :]
-            half = dot_nt(q2[j, tile], k2[j])
-            weights = silu_of_double(half).astype(BF)
-            weights = jnp.concatenate([weights[:TR] * reads_t, weights[TR:] * reads_t], axis=0)
-            out = dot(weights, v2[j])
-            one = um[tile * TR : (tile + 1) * TR, :] > 0.5
-            top = jnp.where(one, out[:TR, 128:], out[:TR, :128])
-            bottom = jnp.where(one, out[TR:, 128:], out[TR:, :128])
-            got_c = jnp.where(first_r, top, bottom) * (1.0 / math.sqrt(HIST))
-            cr[j, tile * TR : (tile + 1) * TR, :] = got_c.astype(BF)
-        return carry
-
-    lax.fori_loop(0, K, cross_pair, 0)
+    make_kv(0, core)
+    gather_rest(A_STATE, sall)
+    make_kv(1, 1 - core)
+
+    def cross_pair(j, tile):
+        tile_rows = pl.ds(pl.multiple_of(tile * TR, TR), TR)
+        reads_t = mb[tile_rows, :]
+        weights = silu_of_double(dot(q2[j, tile], k2[j])).astype(BF)
+        weights = jnp.concatenate([weights[:TR] * reads_t, weights[TR:] * reads_t], axis=0)
+        out = dot(weights, v2[j])
+        one = um[tile_rows, :] > 0.5
+        top = jnp.where(one, out[:TR, 128:], out[:TR, :128])
+        bottom = jnp.where(one, out[TR:, 128:], out[TR:, :128])
+        return jnp.where(first_r, top, bottom)
 
     gather_rest(A_CO, wco_all)
     gather_rest(A_MLP, wm_all)
     gather_rest(A_SCORE, ws_all)
     locals_[3].wait()
     locals_[4].wait()
-    mixed = call[...].reshape(R, 256).astype(F32)
-    for m in range(X):
-        pair = jnp.concatenate([cr[2 * m], cr[2 * m + 1]], axis=1)
-        mixed += dot(pair, wco_all[2 * m : 2 * m + 2].reshape(256, 256))
-    mixed = mixed.astype(BF)
-    total_s = jnp.zeros((R, 128), F32)
-    for m in range(X):
-        half = dot(mixed, jnp.concatenate([wm_all[2 * m], wm_all[2 * m + 1]], axis=1)) * 0.5
-        hidden = silu_of_double(half).astype(BF).astype(F32)
-        total_s += hidden[:, :128] * ws_all[2 * m][0:1, :] + hidden[:, 128:] * ws_all[2 * m + 1][0:1, :]
-    score = jnp.sum(total_s, axis=1, keepdims=True)
-    at_lane = (iota((R, 128), 0) & 15) == (iota((R, 128), 1) & 15)
-    by_slot = jnp.sum(jnp.where(at_lane, score, 0.0).reshape(T, 16, 128), axis=1)
-    sr[...] = by_slot.reshape(T, 1, 128)
+    at_lane = (iota((TR, 128), 0) & 15) == (iota((TR, 128), 1) & 15)
+    SLOTS = TR // 16
+
+    def finish_tile(tile, carry):
+        mixed = call[pl.ds(tile * SLOTS, SLOTS)].reshape(TR, 256).astype(F32)
+        for m in range(X):
+            pair = [
+                (cross_pair(j, tile) * (1.0 / math.sqrt(HIST))).astype(BF)
+                for j in (2 * m, 2 * m + 1)
+            ]
+            mixed += dot(jnp.concatenate(pair, axis=1), wco_all[2 * m : 2 * m + 2].reshape(256, 256))
+        mixed = mixed.astype(BF)
+        total_s = jnp.zeros((TR, 128), F32)
+        for m in range(X):
+            half = dot(mixed, jnp.concatenate([wm_all[2 * m], wm_all[2 * m + 1]], axis=1)) * 0.5
+            hidden = silu_of_double(half).astype(BF).astype(F32)
+            total_s += hidden[:, :128] * ws_all[2 * m][0:1, :] + hidden[:, 128:] * ws_all[2 * m + 1][0:1, :]
+        score = jnp.sum(total_s, axis=1, keepdims=True)
+        by_slot = jnp.sum(jnp.where(at_lane, score, 0.0).reshape(SLOTS, 16, 128), axis=1)
+        sr[pl.ds(tile * SLOTS, SLOTS)] = by_slot.reshape(SLOTS, 1, 128)
+        for i in range(SLOTS):
+            slot = tile * SLOTS + i
+
+            @pl.when(slot != t)
+            def _():
+                pltpu.make_async_remote_copy(
+                    src_ref=sr.at[slot],
+                    dst_ref=rr.at[t],
+                    send_sem=tsend.at[S_SCORE, slot],
+                    recv_sem=trecv.at[S_SCORE, t],
+                    device_id=(slot, k),
+                    device_id_type=MESH,
+                ).start()
+
+        return carry
+
+    lax.fori_loop(0, NT, finish_tile, 0)
     rr[t] = sr[t]
-    over_table(S_SCORE, lambda peer: sr.at[peer], rr)
     table_wait(S_SCORE, rr, False)
     back = rr[...].reshape(T, 128)
     groups = iota((T, 128), 0)
@@ -530,20 +631,15 @@
     table_wait(S_REPLY, replies, True)
     table_wait(S_CAND, call, True)
     table_wait(S_SCORE, rr, True)
-    for a, buf in (
-        (A_OUT, wo_all),
-        (A_KV, wkv_all),
-        (A_CQ, wcq_all),
-        (A_CO, wco_all),
-        (A_MLP, wm_all),
-        (A_SCORE, ws_all),
-        (A_NORM, nall),
-        (A_STATE, sall),
-    ):
-        gather_drain(a, buf)
-    for u in range(2):
-        for d in range(1, K):
-            gated_copy(u, lax.rem(k + d, K), k).wait_send()
+    for a, buf in ((A_OUT, wo_all), (A_K, wk_all), (A_V, wv_all), (A_CQ, wcq_all), (A_CO, wco_all), (A_MLP, wm_all)):
+        relay_drain(a, buf)
+    gather_drain(A_SCORE, ws_all)
+    gather_drain(A_STATE, sall)
+    pair_copy(0, wperm, core).wait_send()
+    pair_copy(1, gains, core).wait_send()
+    for n in range(1, K):
+        normed_copy(others(n), k).wait_send()
+        gated_copy(others(n), k).wait_send()
     for d in range(1, K):
         score_copy(lax.rem(k + d, K), k, d).wait_send()
     for d in range(1, K):
@@ -578,7 +674,7 @@
     slab = table_rows.shape[0]
     cap = max(1, 2 * hist_owner.size // T)
     rows, hist = 16 * T, 64 * K
-    tile = min(rows, 128)
+    tile = min(rows, 256)
     vmem, hbm = pl.BlockSpec(memory_space=pltpu.VMEM), pl.BlockSpec(memory_space=pltpu.HBM)
     scratch = [
         pltpu.SMEM((4,), I32),
@@ -599,28 +695,30 @@
         pltpu.VMEM((T, 2 * cap, 128), BF),
         pltpu.VMEM((T, 16, 256), BF),
         pltpu.VMEM((T, 16, 256), BF),
-        pltpu.VMEM((256, 512), BF),
+        pltpu.VMEM((2, 256, 512), BF),
+        pltpu.VMEM((2, 1, 128), F32),
         pltpu.VMEM((K, 128, 256), BF),
-        pltpu.VMEM((K, 256, 256), BF),
+        pltpu.VMEM((K, 128, 256), BF),
+        pltpu.VMEM((K, 256, 128), BF),
         pltpu.VMEM((K, 128, 256), BF),
         pltpu.VMEM((K, 128, 256), BF),
         pltpu.VMEM((K, 256, 128), BF),
         pltpu.VMEM((K, 8, 128), F32),
         pltpu.VMEM((128, 256), F32),
-        pltpu.VMEM((K, 128, 256), BF),
+        pltpu.VMEM((2, 64, 256), BF),
+        pltpu.VMEM((K, 64, 256), BF),
         pltpu.VMEM((2, hist, 128), BF),
         pltpu.VMEM((2, hist, 128), BF),
         pltpu.VMEM((2, hist, 128), BF),
         pltpu.VMEM((2, hist, 128), BF),
-        pltpu.VMEM((2, K, 64, 128), BF),
-        pltpu.VMEM((2, K, 64, 128), BF),
+        pltpu.VMEM((K, 64, 256), BF),
+        pltpu.VMEM((2, K // 2, 64, 256), BF),
         pltpu.VMEM((K, 128, 256), BF),
         pltpu.VMEM((K, rows // tile, 2 * tile, 256), BF),
-        pltpu.VMEM((K, hist, 256), BF),
+        pltpu.VMEM((K, 256, hist), BF),
         pltpu.VMEM((K, hist, 256), BF),
         pltpu.VMEM((rows, hist), BF),
         pltpu.VMEM((rows, 128), F32),
-        pltpu.VMEM((K, rows, 128), BF),
         pltpu.VMEM((T, 1, 128), F32),
         pltpu.VMEM((T, 1, 128), F32),
         pltpu.VMEM((K, 4, 128), F32),
@@ -629,8 +727,13 @@
         pltpu.SemaphoreType.DMA((4, T)),
         pltpu.SemaphoreType.DMA((8, K)),
         pltpu.SemaphoreType.DMA((8, K)),
-        pltpu.SemaphoreType.DMA((2, K)),
-        pltpu.SemaphoreType.DMA((2, K)),
+        pltpu.SemaphoreType.DMA((8, 2)),
+        pltpu.SemaphoreType.DMA((2,)),
+        pltpu.SemaphoreType.DMA((2,)),
+        pltpu.SemaphoreType.DMA((K,)),
+        pltpu.SemaphoreType.DMA((K,)),
+        pltpu.SemaphoreType.DMA((K,)),
+        pltpu.SemaphoreType.DMA((K,)),
         pltpu.SemaphoreType.DMA((K,)),
         pltpu.SemaphoreType.DMA((K,)),
     ]

time: 79.4 us -> 69.7 us (0.88)
  the two profiles are of different devices: /device:TPU:1 before, /device:TPU:25 now
where the time goes in v3:
time: 69.7 us; the launch traced here: 69.5 us
  Pallas kernels  66.2 us (95%)
  local copies, waits for them, and re-layouts  2.72 us (4%)
    pallas_call x1, Pallas kernels, body(): pl.pallas_call(functools.partial(kernel, T, K, slab, cap), out_shape=(jax...  66.2 us
    unnamed x2, local copies, waits for them, and re-layouts  2.72 us

profile of v3, /device:TPU:25, one launch (start us, length us, event | category | flops | bytes accessed | tf_op | source)
XLA Modules:
  0.0 69.5 jit_solution(4009402409610591026)
XLA Ops:
  0.6 66.2 %shard_map.167 = (bf16[2,64,256]{2,1,0:T(8,128)(2,1)}, f32[4,128]{1,0:T(4,128)}) custom-call(s32[4]{0:T(128)} %group_hbm.1, s32[4]{0:T(128)} %member_hbm.1, s32[4,4]{1,0:T(4,128)} %mask_hbm.1, s32[2,64]{1,0:T(2,128)} %owner_hbm.1, s32[2,64]{1,0:T(2,128)} %row_hbm.1, f32[1,256]{1,0:T(1,128)} %bitcast.12, bf16[256,2,256]{2,1,0:T(2,128)(2,1)} %wproj_hbm.1, ...), custom_call_target="tpu_custom_call" | custom-call | tf_op jit(solution)/shard_map/pallas_call | solution.py:740
  66.8 1.5 %copy.20 = bf16[2,64,256]{2,1,0:T(8,128)(2,1)} copy(bf16[2,64,256]{2,1,0:T(8,128)(2,1)} %get-tuple-element.8) | data formatting | bytes 131072
  68.3 1.2 %copy.21 = f32[512]{0:T(512)} copy(f32[512]{0:T(512)} %bitcast.11) | data formatting | bytes 4096

commit v4 on v3

--- a/solution.py
+++ b/solution.py
@@ -97,7 +97,6 @@
     um,
     sr,
     rr,
-    sc,
     lsem,
     tsend,
     trecv,
@@ -110,19 +109,21 @@
     nrecv,
     gsend,
     grecv,
-    fsend,
-    frecv,
 ):
     t, k = lax.axis_index("table"), lax.axis_index("tensor")
     X = K // 2
     x, core = k // 2, k % 2
     sib = k + 1 - 2 * core
     HIST = 64 * K
-    R = T * 16
+    SL = T // K
     CB = 16 * K
+    R = SL * CB
+    home = t // SL
     TR = min(R, 256)
     NT = R // TR
+    SLOTS = TR // CB
     SHIFT = SLAB.bit_length() - 1
+    assert T == SL * K
 
     def local(i, src, dst):
         return pltpu.make_async_copy(src, dst, lsem.at[i])
@@ -161,6 +162,15 @@
         return carry
 
     lax.fori_loop(1, T, greet, 0)
+
+    def greet_home(g, carry):
+        @pl.when((g != t) | (k != home))
+        def _():
+            pl.semaphore_signal(barrier, inc=1, device_id=(g, home), device_id_type=MESH)
+
+        return carry
+
+    lax.fori_loop(0, T, greet_home, 0)
     for d in range(1, K):
         pl.semaphore_signal(barrier, inc=1, device_id=(t, lax.rem(k + d, K)), device_id_type=MESH)
 
@@ -303,7 +313,7 @@
     msg[1:2, :] = meta
     m1[t] = msg[...]
 
-    pl.semaphore_wait(barrier, T - 1 + K - 1)
+    pl.semaphore_wait(barrier, T - 1 + K - 1 + T - 1 + (k != home).astype(I32))
     over_table(S_MSG, lambda peer: msg, m1)
 
     relay_start(A_OUT, wout_hbm, wo_all)
@@ -372,32 +382,56 @@
 
     for c in late_in:
         c.wait()
-    mine_c = jnp.concatenate(
-        [cand_ref[pl.ds(pl.multiple_of(b * CB + 16 * k, 16), 16), :] for b in range(4)], axis=0
-    )
-    row_c, col_c = iota((R, 64), 0), iota((R, 64), 1)
-    col_group = jnp.zeros((R, 64), I32)
-    for b in range(4):
-        col_group = jnp.where((col_c >> 4) == b, group_s[b], col_group)
-    pick_c = ((row_c >> 4) == col_group) & ((row_c & 15) == (col_c & 15))
-    csend[...] = dot(pick_c.astype(BF), mine_c).astype(BF).reshape(T, 16, 256)
-    call[t] = csend[t]
-
-    metas = m1[:, 1, :].astype(F32)
+
+    @pl.when(k == home)
+    def _():
+        blocks = [cand_ref[b * CB : (b + 1) * CB, :] for b in range(4)]
+
+        def fill(g, carry):
+            block = jnp.zeros((CB, 256), BF)
+            for b in range(4):
+                block = jnp.where(group_s[b] == g, blocks[b], block)
+            csend[g] = block
+            return carry
+
+        lax.fori_loop(0, T, fill, 0)
+        call[t - SL * k] = csend[t]
+
+    def cand_copy(peer, source):
+        return pltpu.make_async_remote_copy(
+            src_ref=csend.at[peer],
+            dst_ref=call.at[source - SL * k],
+            send_sem=tsend.at[S_CAND, peer],
+            recv_sem=trecv.at[S_CAND, source],
+            device_id=(peer, k),
+            device_id_type=MESH,
+        )
+
+    def cand_all(action):
+        @pl.when(k == home)
+        def _():
+            def one(d, carry):
+                action(cand_copy(lax.rem(t + d, T), t))
+                return carry
+
+            lax.fori_loop(1, T, one, 0)
+
+    metas = m1[pl.ds(SL * k, SL), 1, :].astype(F32)
+    lane_s = iota((SL, 128), 1)
 
     def meta_lane(n):
-        return jnp.sum(jnp.where(lane_t == n, metas, 0.0), axis=1, keepdims=True)
+        return jnp.sum(jnp.where(lane_s == n, metas, 0.0), axis=1, keepdims=True)
 
     here = [(meta_lane(b) == t.astype(F32)).astype(F32) for b in range(4)]
     member = sum(here[b] * meta_lane(4 + b) for b in range(4))
     reads = [sum(here[b] * meta_lane(8 + 4 * b + q) for b in range(4)) for q in range(4)]
-    by_row = (iota((R, T), 0) >> 4 == iota((R, T), 1)).astype(BF)
-    um[...] = dot(by_row, jnp.broadcast_to(member, (T, 128)).astype(BF))
-    part = (iota((T, HIST), 1) % (HIST // 2)) // (HIST // 8)
-    reads_wide = jnp.zeros((T, HIST), F32)
+    part = (iota((SL, HIST), 1) % (HIST // 2)) // (HIST // 8)
+    reads_wide = jnp.zeros((SL, HIST), F32)
     for q in range(4):
         reads_wide = jnp.where(part == q, reads[q], reads_wide)
-    mb[...] = dot(by_row, reads_wide.astype(BF)).astype(BF)
+    for i in range(SL):
+        um[i * CB : (i + 1) * CB, :] = jnp.broadcast_to(member[i : i + 1], (CB, 128))
+        mb[i * CB : (i + 1) * CB, :] = jnp.broadcast_to(reads_wide[i : i + 1], (CB, HIST)).astype(BF)
 
     table_wait(S_REPLY, replies, False)
     got = replies[...].reshape(T * 2 * CAP, 128)
@@ -425,16 +459,21 @@
     for n in range(1, K):
         normed_copy(others(n), k).start()
     nall[k] = nown[core]
-    over_table(S_CAND, lambda peer: csend.at[peer], call)
+    cand_all(lambda copy: copy.start())
     pair_copy(0, wperm, 1 - core).wait_recv()
     pair_copy(1, gains, 1 - core).wait_recv()
+
+    first = iota((128, 128), 1) < 64
+    same_half = jnp.where((iota((128, 128), 0) < 64) == first, 1.0 / 64, 0.0).astype(BF)
 
     def project(chip):
         rows_n = nall[pl.ds(2 * chip, 2)].reshape(128, 256)
         place = pl.ds(pl.multiple_of(chip * 128, 128), 128)
         for p in range(2):
             out = silu_of_double(dot(rows_n, wperm[p])).astype(BF)
-            for n, ref in enumerate((pg, pv, pq, pk)):
+            values = out[:, 128:256]
+            pv[p, place, :] = (values.astype(F32) - dot(values, same_half)).astype(BF)
+            for n, ref in ((0, pg), (2, pq), (3, pk)):
                 ref[p, place, :] = out[:, 128 * n : 128 * n + 128]
 
     normed_copy(sib, sib).wait_recv()
@@ -453,9 +492,6 @@
     for n in range(X - 1):
         gather_pass(A_SCORE, ws_all, n)
 
-    lane = iota((128, 128), 1)
-    first = lane < 64
-    same_half = jnp.where((iota((128, 128), 0) < 64) == first, 1.0 / 64, 0.0).astype(BF)
     causal = (iota((256, 128), 0) & 127) >= iota((256, 128), 1)
     zero = jnp.zeros((128, 128), BF)
 
@@ -469,27 +505,25 @@
             device_id_type=MESH,
         )
 
-    for block in range(HIST // 128):
-        start = block * 128
-        for p in range(2):
-            queries = pq[p, start : start + 128, :] * 0.0625
-            both = jnp.concatenate([jnp.where(first, queries, zero), jnp.where(first, zero, queries)], axis=0)
-            half = dot_nt(both, pk[p, start : start + 128, :])
-            weights = jnp.where(causal, silu_of_double(half), 0.0).astype(BF)
-            total = dot(weights, pv[p, start : start + 128, :])
-            if block:
-                weights = silu_of_double(dot_nt(both, pk[p, :start, :])).astype(BF)
-                total += dot(weights, pv[p, :start, :])
-            attended = jnp.where(first, total[:128], total[128:])
-            coarse = attended.astype(BF)
-            fine = (attended - coarse.astype(F32)).astype(BF)
-            off = attended - (dot(coarse, same_half) + dot(fine, same_half))
-            spread_a = dot((off * off).astype(BF), same_half)
-            gate = pg[p, start : start + 128, :].astype(F32)
-            gated = (off * lax.rsqrt(spread_a + 1e-5) * gains[p] * gate).astype(BF)
-            gs[2 * block, :, 128 * p : 128 * p + 128] = gated[:64]
-            gs[2 * block + 1, :, 128 * p : 128 * p + 128] = gated[64:]
-        for dest in (2 * block, 2 * block + 1):
+    for group in ((0, 1), (2, 3)):
+        for block in group:
+            start = block * 128
+            for p in range(2):
+                queries = pq[p, start : start + 128, :] * 0.0625
+                both = jnp.concatenate([jnp.where(first, queries, zero), jnp.where(first, zero, queries)], axis=0)
+                half = dot_nt(both, pk[p, start : start + 128, :])
+                weights = jnp.where(causal, silu_of_double(half), 0.0).astype(BF)
+                total = dot(weights, pv[p, start : start + 128, :])
+                if block:
+                    weights = silu_of_double(dot_nt(both, pk[p, :start, :])).astype(BF)
+                    total += dot(weights, pv[p, :start, :])
+                off = jnp.where(first, total[:128], total[128:])
+                spread_a = dot((off * off).astype(BF), same_half)
+                gate = pg[p, start : start + 128, :].astype(F32)
+                gated = (off * lax.rsqrt(spread_a + 1e-5) * gains[p] * gate).astype(BF)
+                gs[2 * block, :, 128 * p : 128 * p + 128] = gated[:64]
+                gs[2 * block + 1, :, 128 * p : 128 * p + 128] = gated[64:]
+        for dest in [2 * block + half for block in group for half in range(2)]:
 
             @pl.when(k != dest)
             def _():
@@ -498,7 +532,12 @@
     gall[core, x] = gs[k]
 
     relay_finish(A_CQ, wcq_all)
-    table_wait(S_CAND, call, False)
+    for i in range(SL):
+
+        @pl.when(SL * k + i != t)
+        def _():
+            cand_copy(t, SL * k + i).wait_recv()
+
     gather_rest(A_CQ, wcq_all)
     locals_[2].wait()
     first_r = iota((TR, 128), 1) < 64
@@ -506,7 +545,7 @@
 
     def make_queries(j, carry):
         for tile in range(NT):
-            cands = call[tile * (TR // 16) : (tile + 1) * (TR // 16)].reshape(TR, 256)
+            cands = call[tile * SLOTS : (tile + 1) * SLOTS].reshape(TR, 256)
             queries = dot_nt(cands, wcq_all[j]).astype(BF) * 0.0625
             one = um[tile * TR : (tile + 1) * TR, :] > 0.5
             parts = (jnp.where(one, zero_r, queries), jnp.where(one, queries, zero_r))
@@ -569,8 +608,7 @@
     gather_rest(A_SCORE, ws_all)
     locals_[3].wait()
     locals_[4].wait()
-    at_lane = (iota((TR, 128), 0) & 15) == (iota((TR, 128), 1) & 15)
-    SLOTS = TR // 16
+    at_lane = iota((TR, 128), 0) % CB == iota((TR, 128), 1)
 
     def finish_tile(tile, carry):
         mixed = call[pl.ds(tile * SLOTS, SLOTS)].reshape(TR, 256).astype(F32)
@@ -587,50 +625,37 @@
             hidden = silu_of_double(half).astype(BF).astype(F32)
             total_s += hidden[:, :128] * ws_all[2 * m][0:1, :] + hidden[:, 128:] * ws_all[2 * m + 1][0:1, :]
         score = jnp.sum(total_s, axis=1, keepdims=True)
-        by_slot = jnp.sum(jnp.where(at_lane, score, 0.0).reshape(SLOTS, 16, 128), axis=1)
+        by_slot = jnp.sum(jnp.where(at_lane, score, 0.0).reshape(SLOTS, CB, 128), axis=1)
         sr[pl.ds(tile * SLOTS, SLOTS)] = by_slot.reshape(SLOTS, 1, 128)
         for i in range(SLOTS):
-            slot = tile * SLOTS + i
-
-            @pl.when(slot != t)
-            def _():
-                pltpu.make_async_remote_copy(
-                    src_ref=sr.at[slot],
-                    dst_ref=rr.at[t],
-                    send_sem=tsend.at[S_SCORE, slot],
-                    recv_sem=trecv.at[S_SCORE, t],
-                    device_id=(slot, k),
-                    device_id_type=MESH,
-                ).start()
-
+            for j in range(K):
+                score_send(tile * SLOTS + i, j, lambda copy: copy.start())
         return carry
 
-    lax.fori_loop(0, NT, finish_tile, 0)
-    rr[t] = sr[t]
-    table_wait(S_SCORE, rr, False)
-    back = rr[...].reshape(T, 128)
-    groups = iota((T, 128), 0)
-    own_lanes = (lane1 >> 4) == k
-    blocks = [jnp.sum(jnp.where(groups == group_s[b], back, 0.0), axis=0, keepdims=True) for b in range(4)]
-    sc[k] = jnp.where(own_lanes, jnp.concatenate(blocks, axis=0), 0.0)
-
-    def score_copy(dest, source, slot):
+    def score_copy(slot, j, source):
         return pltpu.make_async_remote_copy(
-            src_ref=sc.at[source],
-            dst_ref=sc.at[source],
-            send_sem=fsend.at[slot],
-            recv_sem=frecv.at[source],
-            device_id=(t, dest),
+            src_ref=sr.at[slot],
+            dst_ref=rr.at[source],
+            send_sem=tsend.at[S_SCORE, slot * K + j],
+            recv_sem=trecv.at[S_SCORE, source],
+            device_id=(SL * k + slot, j),
             device_id_type=MESH,
         )
 
-    for d in range(1, K):
-        score_copy(lax.rem(k + d, K), k, d).start()
+    def score_send(slot, j, action):
+        @pl.when((SL * k + slot != t) | (j != k))
+        def _():
+            action(score_copy(slot, j, t))
+
+    lax.fori_loop(0, NT, finish_tile, 0)
+
+    @pl.when(k == home)
+    def _():
+        rr[t] = sr[t - SL * k]
 
     table_wait(S_MSG, m1, True)
     table_wait(S_REPLY, replies, True)
-    table_wait(S_CAND, call, True)
-    table_wait(S_SCORE, rr, True)
+    cand_all(lambda copy: copy.wait_send())
     for a, buf in ((A_OUT, wo_all), (A_K, wk_all), (A_V, wv_all), (A_CQ, wcq_all), (A_CO, wco_all), (A_MLP, wm_all)):
         relay_drain(a, buf)
     gather_drain(A_SCORE, ws_all)
@@ -640,15 +665,22 @@
     for n in range(1, K):
         normed_copy(others(n), k).wait_send()
         gated_copy(others(n), k).wait_send()
-    for d in range(1, K):
-        score_copy(lax.rem(k + d, K), k, d).wait_send()
-    for d in range(1, K):
-        source = lax.rem(k + K - d, K)
-        score_copy(source, source, d).wait_recv()
-    final = sc[0]
-    for n in range(1, K):
-        final += sc[n]
-    scores_ref[...] = final
+
+    def score_wait(g, carry):
+        @pl.when((g != t) | (k != home))
+        def _():
+            score_copy(0, 0, g).wait_recv()
+
+        return carry
+
+    lax.fori_loop(0, T, score_wait, 0)
+    back = rr[...].reshape(T, 128)
+    groups = iota((T, 128), 0)
+    for b in range(4):
+        scores_ref[b : b + 1, :] = jnp.sum(jnp.where(groups == group_s[b], back, 0.0), axis=0, keepdims=True)
+    for slot in range(SL):
+        for j in range(K):
+            score_send(slot, j, lambda copy: copy.wait_send())
 
 
 def body(
@@ -693,8 +725,8 @@
         pltpu.VMEM((T, 2, 128), I32),
         pltpu.VMEM((T, 2 * cap, 128), BF),
         pltpu.VMEM((T, 2 * cap, 128), BF),
-        pltpu.VMEM((T, 16, 256), BF),
-        pltpu.VMEM((T, 16, 256), BF),
+        pltpu.VMEM((T, 16 * K, 256), BF),
+        pltpu.VMEM((T // K, 16 * K, 256), BF),
         pltpu.VMEM((2, 256, 512), BF),
         pltpu.VMEM((2, 1, 128), F32),
         pltpu.VMEM((K, 128, 256), BF),
@@ -719,9 +751,8 @@
         pltpu.VMEM((K, hist, 256), BF),
         pltpu.VMEM((rows, hist), BF),
         pltpu.VMEM((rows, 128), F32),
+        pltpu.VMEM((T // K, 1, 128), F32),
         pltpu.VMEM((T, 1, 128), F32),
-        pltpu.VMEM((T, 1, 128), F32),
-        pltpu.VMEM((K, 4, 128), F32),
         pltpu.SemaphoreType.DMA((16,)),
         pltpu.SemaphoreType.DMA((4, T)),
         pltpu.SemaphoreType.DMA((4, T)),
@@ -730,8 +761,6 @@
         pltpu.SemaphoreType.DMA((8, 2)),
         pltpu.SemaphoreType.DMA((2,)),
         pltpu.SemaphoreType.DMA((2,)),
-        pltpu.SemaphoreType.DMA((K,)),
-        pltpu.SemaphoreType.DMA((K,)),
         pltpu.SemaphoreType.DMA((K,)),
         pltpu.SemaphoreType.DMA((K,)),
         pltpu.SemaphoreType.DMA((K,)),

time: 69.7 us -> 80.7 us (1.16)
  the two profiles are of different devices: /device:TPU:25 before, /device:TPU:64 now
where the time goes in v4:
time: 80.7 us; the launch traced here: 80.6 us
  Pallas kernels  77.2 us (96%)
  local copies, waits for them, and re-layouts  2.72 us (3%)
    pallas_call x1, Pallas kernels, body(): pl.pallas_call(functools.partial(kernel, T, K, slab, cap), out_shape=(jax...  77.2 us
    unnamed x2, local copies, waits for them, and re-layouts  2.72 us

profile of v4, /device:TPU:64, one launch (start us, length us, event | category | flops | bytes accessed | tf_op | source)
XLA Modules:
  0.0 80.6 jit_solution(17854562105209354531)
XLA Ops:
  0.6 77.2 %shard_map.167 = (bf16[2,64,256]{2,1,0:T(8,128)(2,1)}, f32[4,128]{1,0:T(4,128)}) custom-call(s32[4]{0:T(128)} %group_hbm.1, s32[4]{0:T(128)} %member_hbm.1, s32[4,4]{1,0:T(4,128)} %mask_hbm.1, s32[2,64]{1,0:T(2,128)} %owner_hbm.1, s32[2,64]{1,0:T(2,128)} %row_hbm.1, f32[1,256]{1,0:T(1,128)} %bitcast.12, bf16[256,2,256]{2,1,0:T(2,128)(2,1)} %wproj_hbm.1, ...), custom_call_target="tpu_custom_call" | custom-call | tf_op jit(solution)/shard_map/pallas_call | solution.py:769
  77.9 1.5 %copy.20 = bf16[2,64,256]{2,1,0:T(8,128)(2,1)} copy(bf16[2,64,256]{2,1,0:T(8,128)(2,1)} %get-tuple-element.8) | data formatting | bytes 131072
  79.4 1.2 %copy.21 = f32[512]{0:T(512)} copy(f32[512]{0:T(512)} %bitcast.11) | data formatting | bytes 4096

commit v5 on v4

--- a/solution.py
+++ b/solution.py
@@ -70,6 +70,7 @@
     rep,
     replies,
     csend,
+    cin,
     call,
     wperm,
     gains,
@@ -103,6 +104,7 @@
     asend,
     arecv,
     hrecv,
+    crecv,
     psend,
     precv,
     nsend,
@@ -149,10 +151,10 @@
         local(15, ngain_hbm, ngain_ref),
     ]
     late_in = [
-        local(13, cand_hbm, cand_ref),
         local(14, lngain_hbm, lngain_ref),
     ]
-    for c in ids_in + weights_in + locals_ + late_in:
+    cand_in = local(13, cand_hbm, cand_ref)
+    for c in ids_in + weights_in + [cand_in] + locals_ + late_in:
         c.start()
 
     barrier = pltpu.get_barrier_semaphore()
@@ -333,6 +335,30 @@
     pair_copy(0, wperm, core).start()
     pair_copy(1, gains, core).start()
     ws_all[k] = jnp.broadcast_to(wscore_ref[...].astype(F32).reshape(1, 128), (8, 128))
+
+    cand_in.wait()
+    mine_c = jnp.concatenate(
+        [cand_ref[pl.ds(pl.multiple_of(b * CB + 16 * k, 16), 16), :] for b in range(4)], axis=0
+    )
+    row_c, col_c = iota((16 * T, 64), 0), iota((16 * T, 64), 1)
+    col_group = jnp.zeros((16 * T, 64), I32)
+    for b in range(4):
+        col_group = jnp.where((col_c >> 4) == b, group_s[b], col_group)
+    pick_c = ((row_c >> 4) == col_group) & ((row_c & 15) == (col_c & 15))
+    csend[...] = dot(pick_c.astype(BF), mine_c).astype(BF).reshape(T, 16, 256)
+
+    cin[t] = csend[t]
+    over_table(S_CAND, lambda peer: csend.at[peer], cin)
+
+    def cand_copy(dest, source):
+        return pltpu.make_async_remote_copy(
+            src_ref=cin.at[pl.ds(SL * dest, SL)],
+            dst_ref=call.at[:, pl.ds(pl.multiple_of(16 * source, 16), 16)],
+            send_sem=crecv.at[0, dest],
+            recv_sem=crecv.at[1, source],
+            device_id=(t, dest),
+            device_id_type=MESH,
+        )
 
     upper = (iota((128, 128), 0) < iota((128, 128), 1)).astype(BF)
     own_slab = own_row >> SHIFT
@@ -380,41 +406,13 @@
     relay_pass(A_K, wk_all)
     relay_pass(A_V, wv_all)
 
+    table_wait(S_CAND, cin, False)
+    for n in range(1, K):
+        cand_copy(lax.rem(k + n, K), k).start()
+    call[:, pl.ds(pl.multiple_of(16 * k, 16), 16), :] = cin[pl.ds(SL * k, SL)]
+
     for c in late_in:
         c.wait()
-
-    @pl.when(k == home)
-    def _():
-        blocks = [cand_ref[b * CB : (b + 1) * CB, :] for b in range(4)]
-
-        def fill(g, carry):
-            block = jnp.zeros((CB, 256), BF)
-            for b in range(4):
-                block = jnp.where(group_s[b] == g, blocks[b], block)
-            csend[g] = block
-            return carry
-
-        lax.fori_loop(0, T, fill, 0)
-        call[t - SL * k] = csend[t]
-
-    def cand_copy(peer, source):
-        return pltpu.make_async_remote_copy(
-            src_ref=csend.at[peer],
-            dst_ref=call.at[source - SL * k],
-            send_sem=tsend.at[S_CAND, peer],
-            recv_sem=trecv.at[S_CAND, source],
-            device_id=(peer, k),
-            device_id_type=MESH,
-        )
-
-    def cand_all(action):
-        @pl.when(k == home)
-        def _():
-            def one(d, carry):
-                action(cand_copy(lax.rem(t + d, T), t))
-                return carry
-
-            lax.fori_loop(1, T, one, 0)
 
     metas = m1[pl.ds(SL * k, SL), 1, :].astype(F32)
     lane_s = iota((SL, 128), 1)
@@ -459,7 +457,6 @@
     for n in range(1, K):
         normed_copy(others(n), k).start()
     nall[k] = nown[core]
-    cand_all(lambda copy: copy.start())
     pair_copy(0, wperm, 1 - core).wait_recv()
     pair_copy(1, gains, 1 - core).wait_recv()
 
@@ -532,12 +529,8 @@
     gall[core, x] = gs[k]
 
     relay_finish(A_CQ, wcq_all)
-    for i in range(SL):
-
-        @pl.when(SL * k + i != t)
-        def _():
-            cand_copy(t, SL * k + i).wait_recv()
-
+    for n in range(1, K):
+        cand_copy(others(n), others(n)).wait_recv()
     gather_rest(A_CQ, wcq_all)
     locals_[2].wait()
     first_r = iota((TR, 128), 1) < 64
@@ -655,7 +648,9 @@
 
     table_wait(S_MSG, m1, True)
     table_wait(S_REPLY, replies, True)
-    cand_all(lambda copy: copy.wait_send())
+    table_wait(S_CAND, cin, True)
+    for n in range(1, K):
+        cand_copy(others(n), k).wait_send()
     for a, buf in ((A_OUT, wo_all), (A_K, wk_all), (A_V, wv_all), (A_CQ, wcq_all), (A_CO, wco_all), (A_MLP, wm_all)):
         relay_drain(a, buf)
     gather_drain(A_SCORE, ws_all)
@@ -725,7 +720,8 @@
         pltpu.VMEM((T, 2, 128), I32),
         pltpu.VMEM((T, 2 * cap, 128), BF),
         pltpu.VMEM((T, 2 * cap, 128), BF),
-        pltpu.VMEM((T, 16 * K, 256), BF),
+        pltpu.VMEM((T, 16, 256), BF),
+        pltpu.VMEM((T, 16, 256), BF),
         pltpu.VMEM((T // K, 16 * K, 256), BF),
         pltpu.VMEM((2, 256, 512), BF),
         pltpu.VMEM((2, 1, 128), F32),
@@ -759,6 +755,7 @@
         pltpu.SemaphoreType.DMA((8, K)),
         pltpu.SemaphoreType.DMA((8, K)),
         pltpu.SemaphoreType.DMA((8, 2)),
+        pltpu.SemaphoreType.DMA((2, K)),
         pltpu.SemaphoreType.DMA((2,)),
         pltpu.SemaphoreType.DMA((2,)),
         pltpu.SemaphoreType.DMA((K,)),

time: 80.7 us -> 67.9 us (0.84)
  the two profiles are of different devices: /device:TPU:64 before, /device:TPU:1 now
where the time goes in v5:
time: 67.9 us; the launch traced here: 66.9 us
  Pallas kernels  63.5 us (94%)
  local copies, waits for them, and re-layouts  2.72 us (4%)
    pallas_call x1, Pallas kernels, body(): pl.pallas_call(functools.partial(kernel, T, K, slab, cap), out_shape=(jax...  63.5 us
    unnamed x2, local copies, waits for them, and re-layouts  2.72 us

profile of v5, /device:TPU:1, one launch (start us, length us, event | category | flops | bytes accessed | tf_op | source)
XLA Modules:
  0.0 66.9 jit_solution(1679533185724575751)
XLA Ops:
  0.6 63.5 %shard_map.167 = (bf16[2,64,256]{2,1,0:T(8,128)(2,1)}, f32[4,128]{1,0:T(4,128)}) custom-call(s32[4]{0:T(128)} %group_hbm.1, s32[4]{0:T(128)} %member_hbm.1, s32[4,4]{1,0:T(4,128)} %mask_hbm.1, s32[2,64]{1,0:T(2,128)} %owner_hbm.1, s32[2,64]{1,0:T(2,128)} %row_hbm.1, f32[1,256]{1,0:T(1,128)} %bitcast.12, bf16[256,2,256]{2,1,0:T(2,128)(2,1)} %wproj_hbm.1, ...), custom_call_target="tpu_custom_call" | custom-call | tf_op jit(solution)/shard_map/pallas_call | solution.py:766
  64.1 1.5 %copy.20 = bf16[2,64,256]{2,1,0:T(8,128)(2,1)} copy(bf16[2,64,256]{2,1,0:T(8,128)(2,1)} %get-tuple-element.8) | data formatting | bytes 131072
  65.6 1.2 %copy.21 = f32[512]{0:T(512)} copy(f32[512]{0:T(512)} %bitcast.11) | data formatting | bytes 4096

commit v6 on v5

--- a/solution.py
+++ b/solution.py
@@ -327,6 +327,9 @@
     wv_all[k] = jnp.concatenate([kv0[:, 64:], kv1[:, 64:]], axis=1)
     relay_start(A_K, wk_all.at[k], wk_all)
     relay_start(A_V, wv_all.at[k], wv_all)
+    relay_start(A_CQ, wcq_hbm, wcq_all)
+    relay_start(A_CO, wco_hbm, wco_all)
+    relay_start(A_MLP, wmlp_hbm, wm_all)
     wproj = wproj_ref[...]
     w0, w1 = wproj[:, 0, :], wproj[:, 1, :]
     half_w = [w[:, 64 * i : 64 * i + 64] for i in range(4) for w in (w0, w1)]
@@ -335,6 +338,7 @@
     pair_copy(0, wperm, core).start()
     pair_copy(1, gains, core).start()
     ws_all[k] = jnp.broadcast_to(wscore_ref[...].astype(F32).reshape(1, 128), (8, 128))
+    gather_start(A_SCORE, ws_all.at[k], ws_all)
 
     cand_in.wait()
     mine_c = jnp.concatenate(
@@ -372,10 +376,6 @@
     pick_right = (spots == slot_col + CAP).astype(BF)
 
     table_wait(S_MSG, m1, False)
-    relay_start(A_CQ, wcq_hbm, wcq_all)
-    relay_start(A_CO, wco_hbm, wco_all)
-    relay_start(A_MLP, wmlp_hbm, wm_all)
-    gather_start(A_SCORE, ws_all.at[k], ws_all)
     wanted_ids = m1[:, 0, :]
     mine = (wanted_ids >> SHIFT) == t
     rank_in = dot(mine.astype(BF), upper)
@@ -394,9 +394,10 @@
     locals_[0].wait()
     CH = min(512, SLAB)
     rows = jnp.zeros((T * CAP, 256), F32)
-    at = iota((T * CAP, CH), 1)
+    in_chunk = (iota((T * CAP, CH), 1) == (want_col & (CH - 1))).astype(BF)
+    of_chunk = want_col // CH
     for c in range(SLAB // CH):
-        rows += dot((at == want_col - c * CH).astype(BF), tab[c * CH : (c + 1) * CH, :])
+        rows += jnp.where(of_chunk == c, dot(in_chunk, tab[c * CH : (c + 1) * CH, :]), 0.0)
     halves = [rows[:, :128].reshape(T, CAP, 128), rows[:, 128:].reshape(T, CAP, 128)]
     rep[...] = jnp.concatenate(halves, axis=1).astype(BF)
     replies[t] = rep[t]

time: 67.9 us -> 67.4 us (level)
  the two profiles are of different devices: /device:TPU:1 before, /device:TPU:64 now
where the time goes in v6:
time: 67.4 us; the launch traced here: 67.2 us
  Pallas kernels  63.9 us (95%)
  local copies, waits for them, and re-layouts  2.72 us (4%)
    pallas_call x1, Pallas kernels, body(): pl.pallas_call(functools.partial(kernel, T, K, slab, cap), out_shape=(jax...  63.9 us
    unnamed x2, local copies, waits for them, and re-layouts  2.72 us

profile of v6, /device:TPU:64, one launch (start us, length us, event | category | flops | bytes accessed | tf_op | source)
XLA Modules:
  0.0 67.2 jit_solution(15964816311861546935)
XLA Ops:
  0.6 63.9 %shard_map.167 = (bf16[2,64,256]{2,1,0:T(8,128)(2,1)}, f32[4,128]{1,0:T(4,128)}) custom-call(s32[4]{0:T(128)} %group_hbm.1, s32[4]{0:T(128)} %member_hbm.1, s32[4,4]{1,0:T(4,128)} %mask_hbm.1, s32[2,64]{1,0:T(2,128)} %owner_hbm.1, s32[2,64]{1,0:T(2,128)} %row_hbm.1, f32[1,256]{1,0:T(1,128)} %bitcast.12, bf16[256,2,256]{2,1,0:T(2,128)(2,1)} %wproj_hbm.1, ...), custom_call_target="tpu_custom_call" | custom-call | tf_op jit(solution)/shard_map/pallas_call | solution.py:767
  64.5 1.5 %copy.20 = bf16[2,64,256]{2,1,0:T(8,128)(2,1)} copy(bf16[2,64,256]{2,1,0:T(8,128)(2,1)} %get-tuple-element.8) | data formatting | bytes 131072
  66.0 1.2 %copy.21 = f32[512]{0:T(512)} copy(f32[512]{0:T(512)} %bitcast.11) | data formatting | bytes 4096
